TPU v7x, 128 devices: a whole 4x4x4 slice. The times are simulated.
128 devices in a mesh: heads: 4 (over y), ctx: 32 (over z, x, core).
Axes of the slice: x: 4, y: 4, z: 4, core: 2. Of those that a mesh axis runs over, the one named last changes fastest.
Arguments:
- queries: bfloat16 [8192, 8192], P(('ctx', 'heads')), may hold values from -120 to 120
- keys: bfloat16 [8192, 1024], P(('ctx', 'heads')), may hold values from -6 to 6
- values: bfloat16 [8192, 1024], P(('ctx', 'heads')), may hold values from -3 to 3
- grad_out: bfloat16 [8192, 8192], P(('ctx', 'heads')), may hold values from -1.5 to 1.5
- doc_lengths: int32 [16], replicated, may hold values from 1 to 1024, 8192 in all
- share_prefix: int32 [16], replicated, may hold values 0 or 1
Outputs:
- attn_out: bfloat16 [8192, 8192], P(('ctx', 'heads'))
- grad_queries: bfloat16 [8192, 8192], P(('ctx', 'heads'))
- grad_keys: bfloat16 [8192, 1024], P(('ctx', 'heads'))
- grad_values: bfloat16 [8192, 1024], P(('ctx', 'heads'))
Inputs may be any that keep to these rules, and one draw needn't show every extreme that they name: `doc_lengths`: they sum to 8192.
All inputs are finite; a program needn't handle non-finite values.
Results may differ from a plain program's by a relative error of at most 0.035.
Values may be sent and summed in bfloat16 or wider, within the bound.
A program may use at most 128 MiB of HBM per device.

v0:
```python
import math

import jax
import jax.numpy as jnp
from jax import lax
from jax.sharding import PartitionSpec as P

QH = 64
KVH = 8
HD = 128


def document_of(pos, ends):
    return jnp.sum((ends[None, :] <= pos[:, None]).astype(jnp.int32), axis=1)


def visible(qpos, qdoc, qshare, kpos, kdoc, usable):
    same = kdoc[None, :] == qdoc[:, None]
    prefix = (kdoc[None, :] == 0) & (qshare[:, None] == 1)
    return (kpos[None, :] <= qpos[:, None]) & (same | prefix) & usable[None, :]


def on_device(queries, keys, values, grad_out, doc_lengths, share_prefix):
    q_loc, k_loc, v_loc, do_loc = (
        lax.all_to_all(queries, "heads", split_axis=1, concat_axis=0, tiled=True),
        lax.all_to_all(keys, "heads", split_axis=1, concat_axis=0, tiled=True),
        lax.all_to_all(values, "heads", split_axis=1, concat_axis=0, tiled=True),
        lax.all_to_all(grad_out, "heads", split_axis=1, concat_axis=0, tiled=True),
    )
    tok = q_loc.shape[0]
    shard = lax.axis_index("ctx")
    kv_width = k_loc.shape[1]
    groups = kv_width // HD
    per = QH // KVH
    scale = HD ** (-0.5)
    ndocs = doc_lengths.shape[0]
    ends = jnp.cumsum(doc_lengths)
    local_rows = jnp.arange(tok, dtype=jnp.int32)
    qpos = shard * tok + local_rows
    qdoc = document_of(qpos, ends)
    qshare = jnp.sum(
        jnp.where(
            qdoc[:, None] == jnp.arange(ndocs, dtype=jnp.int32)[None, :], share_prefix[None, :], 0
        ),
        axis=1,
    )
    q_four = q_loc.reshape(tok, groups, per, HD)
    do_four = do_loc.reshape(tok, groups, per, HD)
    key_set, val_set = (
        lax.all_gather(k_loc, "ctx", axis=0, tiled=True),
        lax.all_gather(v_loc, "ctx", axis=0, tiled=True),
    )
    kpos_set = jnp.arange(key_set.shape[0], dtype=jnp.int32)
    use_set = jnp.ones((key_set.shape[0],), jnp.bool_)
    whole = key_set.shape[0]
    width = math.gcd(whole, 512)
    nblocks = whole // width
    k_stack = key_set.reshape(nblocks, width, kv_width)
    v_stack = val_set.reshape(nblocks, width, kv_width)
    p_stack = kpos_set.reshape(nblocks, width)
    u_stack = use_set.reshape(nblocks, width)

    def forward_step(carry, items):
        k_piece, v_piece, p_piece, u_piece = items
        allowed = visible(qpos, qdoc, qshare, p_piece, document_of(p_piece, ends), u_piece)

        def forward_compute(state):
            top, total, acc = state
            k_blk = k_piece.reshape(width, groups, HD)
            v_blk = v_piece.reshape(width, groups, HD)
            score = (
                jnp.einsum("tgjd,sgd->gjts", q_four, k_blk, preferred_element_type=jnp.float32)
                * scale
            )
            score = jnp.where(allowed[None, None], score, -1e30)
            top_new = jnp.maximum(top, jnp.max(score, axis=-1))
            prob = jnp.where(allowed[None, None], jnp.exp(score - top_new[..., None]), 0.0)
            factor = jnp.exp(top - top_new)
            total = total * factor + jnp.sum(prob, axis=-1)
            weighted = jnp.einsum(
                "gjts,sgd->tgjd",
                prob.astype(jnp.bfloat16),
                v_blk,
                preferred_element_type=jnp.float32,
            )
            acc = acc * jnp.transpose(factor, (2, 0, 1))[..., None] + weighted
            return (top_new, total, acc)

        return (lax.cond(jnp.any(allowed), forward_compute, lambda state: state, carry), None)

    start_state = (
        jnp.full((groups, per, tok), -1e30, jnp.float32),
        jnp.zeros((groups, per, tok), jnp.float32),
        jnp.zeros((tok, groups, per, HD), jnp.float32),
    )
    (top, total, acc), _ = lax.scan(forward_step, start_state, (k_stack, v_stack, p_stack, u_stack))
    out_four = (acc / jnp.transpose(total, (2, 0, 1))[..., None]).astype(jnp.bfloat16)
    lse = top + jnp.log(total)
    delta = jnp.transpose(
        jnp.sum(do_four.astype(jnp.float32) * out_four.astype(jnp.float32), axis=-1), (1, 2, 0)
    )

    def back_step(grad_q, items):
        k_piece, v_piece, p_piece, u_piece = items
        allowed = visible(qpos, qdoc, qshare, p_piece, document_of(p_piece, ends), u_piece)

        def back_compute(state):
            k_blk = k_piece.reshape(width, groups, HD)
            v_blk = v_piece.reshape(width, groups, HD)
            score = (
                jnp.einsum("tgjd,sgd->gjts", q_four, k_blk, preferred_element_type=jnp.float32)
                * scale
            )
            prob = jnp.where(
                allowed[None, None],
                jnp.exp(jnp.where(allowed[None, None], score, -1e30) - lse[..., None]),
                0.0,
            )
            dprob = jnp.einsum("tgjd,sgd->gjts", do_four, v_blk, preferred_element_type=jnp.float32)
            dscore = (prob * (dprob - delta[..., None])).astype(jnp.bfloat16)
            state = (
                state
                + jnp.einsum("gjts,sgd->tgjd", dscore, k_blk, preferred_element_type=jnp.float32)
                * scale
            )
            grad_k = (
                jnp.einsum("gjts,tgjd->sgd", dscore, q_four, preferred_element_type=jnp.float32)
                * scale
            )
            grad_v = jnp.einsum(
                "gjts,tgjd->sgd",
                prob.astype(jnp.bfloat16),
                do_four,
                preferred_element_type=jnp.float32,
            )
            return (state, (grad_k.reshape(width, kv_width), grad_v.reshape(width, kv_width)))

        def passby(state):
            empty = jnp.zeros((width, kv_width), jnp.float32)
            return (state, (empty, empty))

        return lax.cond(jnp.any(allowed), back_compute, passby, grad_q)

    grad_q, (k_terms, v_terms) = lax.scan(
        back_step,
        jnp.zeros((tok, groups, per, HD), jnp.float32),
        (k_stack, v_stack, p_stack, u_stack),
    )
    k_terms = k_terms.reshape(whole, kv_width)
    v_terms = v_terms.reshape(whole, kv_width)
    k_sum, v_sum = (
        lax.psum_scatter(k_terms, "ctx", scatter_dimension=0, tiled=True),
        lax.psum_scatter(v_terms, "ctx", scatter_dimension=0, tiled=True),
    )
    out_rows = out_four.reshape(tok, groups * per * HD)
    dq_rows = grad_q.astype(jnp.bfloat16).reshape(tok, groups * per * HD)
    results = (
        lax.all_to_all(out_rows, "heads", split_axis=0, concat_axis=1, tiled=True),
        lax.all_to_all(dq_rows, "heads", split_axis=0, concat_axis=1, tiled=True),
        lax.all_to_all(
            k_sum.astype(jnp.bfloat16), "heads", split_axis=0, concat_axis=1, tiled=True
        ),
        lax.all_to_all(
            v_sum.astype(jnp.bfloat16), "heads", split_axis=0, concat_axis=1, tiled=True
        ),
    )
    return (results[0], results[1], results[2], results[3])


def solution(mesh):
    in_specs = (
        P(("ctx", "heads"), None),
        P(("ctx", "heads"), None),
        P(("ctx", "heads"), None),
        P(("ctx", "heads"), None),
        P(),
        P(),
    )
    out_specs = (
        P(("ctx", "heads"), None),
        P(("ctx", "heads"), None),
        P(("ctx", "heads"), None),
        P(("ctx", "heads"), None),
    )
    return jax.shard_map(
        on_device, mesh=mesh, in_specs=in_specs, out_specs=out_specs, check_vma=False
    )
```

profile of v0, /device:TPU:2, one launch (start us, length us, event | category | flops | bytes accessed | tf_op | source)
XLA Modules:
  0.0 625.6 jit_solution(10395362050765231305)
XLA Ops:
  8.1 10.3 %all_to_all.146 = bf16[64,4,256]{2,0,1:T(8,128)(2,1)} all-to-all(bf16[64,4,256]{2,0,1:T(8,128)(2,1)S(1)} %bitcast.174), channel_id=1, replica_groups=mesh['heads'=4,'ctx'=32] {'heads'}, dimensions={1} | all-to-all | bytes 262144 | tf_op jit(solution)/shard_map/all_to_all | solution.py:26
  19.5 9.0 %all_to_all.147 = bf16[64,4,256]{2,0,1:T(8,128)(2,1)} all-to-all(bf16[64,4,256]{2,0,1:T(8,128)(2,1)S(1)} %bitcast.175), channel_id=1, replica_groups=mesh['heads'=4,'ctx'=32] {'heads'}, dimensions={1} | all-to-all | bytes 262144 | tf_op jit(solution)/shard_map/all_to_all | solution.py:27
  30.9 3.5 all-to-all-start.1
  36.7 10.4 %all-to-all-done.1 = bf16[64,4,2048]{2,0,1:T(8,128)(2,1)S(1)} async-done(((bf16[64,4,2048]{2,0,1:T(8,128)(2,1)}), bf16[64,4,2048]{2,0,1:T(8,128)(2,1)S(1)}, u32[]{:S(2)}, u32[]{:S(2)}) %all-to-all-start.1) | async-done | bytes 1048608 | tf_op jit(solution)/shard_map/all_to_all | solution.py:25
  47.1 4.3 all-to-all-start.4
  53.2 9.8 %all-to-all-done.4 = bf16[64,4,2048]{2,0,1:T(8,128)(2,1)} async-done(((bf16[64,4,2048]{2,0,1:T(8,128)(2,1)}), bf16[64,4,2048]{2,0,1:T(8,128)(2,1)}, u32[]{:S(2)}, u32[]{:S(2)}) %all-to-all-start.4) | async-done | bytes 1048608 | tf_op jit(solution)/shard_map/all_to_all | solution.py:28
  66.1 6.4 %copy.156 = bf16[16,512,256]{1,2,0:T(8,128)(2,1)} copy(bf16[16,512,256]{2,1,0:T(8,128)(2,1)} %bitcast.159) | data formatting | bytes 8388608
  72.5 40.4 %all-gather.5.cloned.1.call-done = bf16[8192,256]{1,0:T(8,128)(2,1)} async-done(((bf16[256,256]{1,0:T(8,128)(2,1)}), bf16[8192,256]{1,0:T(8,128)(2,1)}) %all-gather.5.cloned.1.call-update) | async-done | bytes 4194320 | tf_op jit(solution)/shard_map/all_gather | solution.py:51
  112.9 6.4 %copy.158 = bf16[16,512,256]{1,2,0:T(8,128)(2,1)} copy(bf16[16,512,256]{2,1,0:T(8,128)(2,1)} %bitcast.160) | data formatting | bytes 8388608
  120.9 45.8 %while.33 = (s32[]{:T(128)}, f32[2,8,256]{2,1,0:T(8,128)S(1)}, f32[2,8,256]{2,1,0:T(8,128)S(1)}, f32[256,2,8,128]{3,0,2,1:T(8,128)}, s32[16,512]{1,0:T(8,128)S(1...) while((s32[]{:T(128)}, f32[2,8,256]{2,1,0:T(8,128)S(1)}, ...), condition=%wide.region_10.11_spmd.clone, body=%wide.region_3.10_spmd.clone.sunk | while | flops 1102877184 | bytes 49565576 | solution.py:96
  122.5 9.5 %conditional.6 = ((f32[2,8,256]{2,1,0:T(8,128)S(1)}, f32[2,8,256]{2,1,0:T(8,128)S(1)}, f32[256,2,8,128]{3,0,2,1:T(8,128)})) conditional(s32[]{:T(128)} %convert_element_type.78, (f32[2,8,256]{2,1,0:T(8,128)S(1)}, f32[2,8,256]{2,1,0:T(8,128)S(1)}, f32[256,2,8,128]{3,0,2,1:T(8,128)}) %tuple.96, (pred[256,512]{0,1:T(8,128)(4,1)S(1)}, ...), branch_computations={%region_6.6_spmd, %region_7.9_spmd} | conditional | flops 1102065664 | bytes 49414236 | solution.py:89
  133.7 9.5 %conditional.6 = ((f32[2,8,256]{2,1,0:T(8,128)S(1)}, f32[2,8,256]{2,1,0:T(8,128)S(1)}, f32[256,2,8,128]{3,0,2,1:T(8,128)})) conditional(s32[]{:T(128)} %convert_element_type.78, (f32[2,8,256]{2,1,0:T(8,128)S(1)}, f32[2,8,256]{2,1,0:T(8,128)S(1)}, f32[256,2,8,128]{3,0,2,1:T(8,128)}) %tuple.96, (pred[256,512]{0,1:T(8,128)(4,1)S(1)}, ...), branch_computations={%region_6.6_spmd, %region_7.9_spmd} | conditional | flops 1102065664 | bytes 49414236 | solution.py:89
  166.9 4.2 multiply_reduce_fusion
  171.4 182.9 %while.34 = (s32[]{:T(128)}, f32[256,2,8,128]{3,0,2,1:T(8,128)S(1)}, f32[16,512,256]{2,1,0:T(8,128)}, f32[16,512,256]{2,1,0:T(8,128)}, s32[16,512]{1,0:T(8,128)S...) while((s32[]{:T(128)}, ...), condition=%wide.region_17.18_spmd.clone, body=%wide.region_12.17_spmd.clone.sunk | while | flops 2711511552 | bytes 57872744 | solution.py:144
  173.3 14.0 %conditional.7 = (f32[256,2,8,128]{3,0,2,1:T(8,128)S(1)}, f32[1,512,256]{1,2,0:T(8,128)}, f32[1,512,256]{1,2,0:T(8,128)}) conditional(s32[]{:T(128)} %convert_element_type.80, f32[256,2,8,128]{3,0,2,1:T(8,128)S(1)} %get-tuple-element.848, (pred[256,512]{0,1:T(8,128)(4,1)S(1)}, bf16[16,512,256]{1,2,0:T(8,128)(2,1)}, s32[]{:T(128)}, ...), branch_computations={%region_15.15_spmd, %region_16.16_spmd} | conditional | flops 2710700032 | bytes 53526584 | solution.py:142
  195.4 13.9 %conditional.7 = (f32[256,2,8,128]{3,0,2,1:T(8,128)S(1)}, f32[1,512,256]{1,2,0:T(8,128)}, f32[1,512,256]{1,2,0:T(8,128)}) conditional(s32[]{:T(128)} %convert_element_type.80, f32[256,2,8,128]{3,0,2,1:T(8,128)S(1)} %get-tuple-element.848, (pred[256,512]{0,1:T(8,128)(4,1)S(1)}, bf16[16,512,256]{1,2,0:T(8,128)(2,1)}, s32[]{:T(128)}, ...), branch_computations={%region_15.15_spmd, %region_16.16_spmd} | conditional | flops 2710700032 | bytes 53526584 | solution.py:142
  197.9 3.5 fusion.22
  356.7 4.3 all-to-all-start.3
  363.1 13.4 %all-to-all-done.3 = bf16[4,64,2048]{2,1,0:T(8,128)(2,1)S(1)} async-done(((bf16[4,64,2048]{2,1,0:T(8,128)(2,1)}), bf16[4,64,2048]{2,1,0:T(8,128)(2,1)S(1)}, u32[]{:S(2)}, u32[]{:S(2)}) %all-to-all-start.3) | async-done | bytes 1048608 | tf_op jit(solution)/shard_map/all_to_all | solution.py:158
  376.5 3.5 all-to-all-start.5
  380.0 130.5 %reduce-scatter.3.cloned.1.call-done = f32[256,256]{1,0:T(8,128)} async-done(((f32[8192,256]{1,0:T(8,128)}), f32[256,256]{1,0:T(8,128)}) %reduce-scatter.3.cloned.1.call-update) | async-done | bytes 262160 | tf_op jit(solution)/shard_map/reduce_scatter | solution.py:152
  512.1 4.3 all-to-all-start.6
  516.4 90.2 %reduce-scatter.5.cloned.1.call-done = f32[256,256]{1,0:T(8,128)} async-done(((f32[8192,256]{1,0:T(8,128)}), f32[256,256]{1,0:T(8,128)}) %reduce-scatter.5.cloned.1.call-update) | async-done | bytes 262160 | tf_op jit(solution)/shard_map/reduce_scatter | solution.py:153
  608.2 4.3 all-to-all-start.7
  (386 shorter events, 256.9 us)
Async XLA Ops:
  7.2 44.3 %copy-start.4 = (s32[16]{0:T(128)S(1)}, s32[16]{0:T(128)}, u32[]{:S(2)}) copy-start(s32[16]{0:T(128)} %param.18) | copy-start | bytes 196
  7.2 44.7 %copy-start.5 = (s32[16]{0:T(128)S(1)}, s32[16]{0:T(128)}, u32[]{:S(2)}) copy-start(s32[16]{0:T(128)} %param.19) | copy-start | bytes 196
  7.2 58.9 %all-gather.3.cloned.1.call-start = ((), (), s32[]{:S(2)}) async-start(), calls=%async_computation.10 | async-start | bytes 4325376 | tf_op jit(solution)/shard_map/all_gather | solution.py:50
  18.5 94.4 %all-gather.5.cloned.1.call-start = ((), (), s32[]{:S(2)}) async-start(), calls=%async_computation.11 | async-start | bytes 4325376 | tf_op jit(solution)/shard_map/all_gather | solution.py:51
  30.9 16.3 %all-to-all-start.1 = ((bf16[64,4,2048]{2,0,1:T(8,128)(2,1)}), bf16[64,4,2048]{2,0,1:T(8,128)(2,1)S(1)}, u32[]{:S(2)}, u32[]{:S(2)}) async-start(bf16[64,4,2048]{2,0,1:T(8,128)(2,1)} %bitcast.141), calls=%async_computation.1 | async-start | bytes 2097152 | tf_op jit(solution)/shard_map/all_to_all | solution.py:25
  47.1 15.9 %all-to-all-start.4 = ((bf16[64,4,2048]{2,0,1:T(8,128)(2,1)}), bf16[64,4,2048]{2,0,1:T(8,128)(2,1)}, u32[]{:S(2)}, u32[]{:S(2)}) async-start(bf16[64,4,2048]{2,0,1:T(8,128)(2,1)} %bitcast.140), calls=%async_computation.4 | async-start | bytes 2097152 | tf_op jit(solution)/shard_map/all_to_all | solution.py:28
  51.4 459.1 %reduce-scatter.3.cloned.1.call-start = ((), (), s32[]{:S(2)}) async-start(), calls=%async_computation.12 | async-start | bytes 8650752 | tf_op jit(solution)/shard_map/reduce_scatter | solution.py:152
  123.6 3.6 copy-start
  130.7 1.4 copy-start.1
  134.8 3.6 copy-start
  141.8 1.4 copy-start.1
  173.3 2.5 copy-start.3
  195.4 2.5 copy-start.3
  354.2 1.2 copy-start.2
  354.2 252.3 %reduce-scatter.5.cloned.1.call-start = ((), (), s32[]{:S(2)}) async-start(), calls=%async_computation.13 | async-start | bytes 8650752 | tf_op jit(solution)/shard_map/reduce_scatter | solution.py:153
  356.7 19.8 %all-to-all-start.3 = ((bf16[4,64,2048]{2,1,0:T(8,128)(2,1)}), bf16[4,64,2048]{2,1,0:T(8,128)(2,1)S(1)}, u32[]{:S(2)}, u32[]{:S(2)}) async-start(bf16[4,64,2048]{2,1,0:T(8,128)(2,1)} %all_to_all.119), calls=%async_computation.3 | async-start | bytes 2097152 | tf_op jit(solution)/shard_map/all_to_all | solution.py:158
  376.5 135.6 %all-to-all-start.5 = ((bf16[4,64,2048]{2,1,0:T(8,128)(2,1)}), bf16[4,64,2048]{2,1,0:T(8,128)(2,1)S(1)}, u32[]{:S(2)}, u32[]{:S(2)}) async-start(bf16[4,64,2048]{2,1,0:T(8,128)(2,1)} %all_to_all.126), calls=%async_computation.5 | async-start | bytes 2097152 | tf_op jit(solution)/shard_map/all_to_all | solution.py:159
  512.1 96.1 %all-to-all-start.6 = ((bf16[4,64,256]{2,1,0:T(8,128)(2,1)}), bf16[4,64,256]{2,1,0:T(8,128)(2,1)S(1)}, u32[]{:S(2)}, u32[]{:S(2)}) async-start(bf16[4,64,256]{2,1,0:T(8,128)(2,1)} %bitcast.37), calls=%async_computation.7 | async-start | bytes 262144 | tf_op jit(solution)/shard_map/all_to_all | solution.py:160
  608.2 10.3 %all-to-all-start.7 = ((bf16[4,64,256]{2,1,0:T(8,128)(2,1)}), bf16[4,64,256]{2,1,0:T(8,128)(2,1)S(1)}, u32[]{:S(2)}, u32[]{:S(2)}) async-start(bf16[4,64,256]{2,1,0:T(8,128)(2,1)} %bitcast.40), calls=%async_computation.9 | async-start | bytes 262144 | tf_op jit(solution)/shard_map/all_to_all | solution.py:163
Sparse Core Ops, SparseCore 0:
  18.6 46.2 all-gather.2
  67.2 45.6 all-gather.4
  354.4 156.1 reduce-scatter.2
  514.5 92.0 reduce-scatter.4
where the time goes:
time: 619 us; the launch traced here: 626 us
  waiting for transfers between devices  298 us (48%)
  local copies, waits for them, and re-layouts  168 us (27%)
  other arithmetic  45.5 us (7%)
  matrix products  35.4 us (6%)
  starting transfers between devices  24.3 us (4%)
  loops' own time  21.2 us (3%)
  blocking collectives  19.4 us (3%)
  between operations  13.9 us (2%)
    reduce_scatter x1, waiting for transfers between devices, on_device(): lax.psum_scatter(k_terms, 'ctx', scatter_dimension=0, tiled=True)  130 us
    dynamic_update_slice x48, local copies, waits for them, and re-layouts, on_device(): lax.scan(back_step, jnp.zeros((tok, groups, per, HD), jnp.float32), (k_st...  102 us
    reduce_scatter x1, waiting for transfers between devices, on_device(): lax.psum_scatter(v_terms, 'ctx', scatter_dimension=0, tiled=True)  90.2 us
    all_gather x1, waiting for transfers between devices, on_device(): lax.all_gather(v_loc, 'ctx', axis=0, tiled=True)  40.4 us
    broadcast_in_dim x28, local copies, waits for them, and re-layouts, on_device(): lax.scan(back_step, jnp.zeros((tok, groups, per, HD), jnp.float32), (k_st...  24.6 us
    unnamed x14, local copies, waits for them, and re-layouts  17.9 us
    reduce_or x16, other arithmetic, back_step(): return lax.cond(jnp.any(allowed), back_compute, passby, grad_q)  15.5 us
    reduce_or x16, other arithmetic, forward_step(): jnp.any(allowed)  14.6 us
  transfers between devices with their start and end apart: 10, of which 7 were waited for; matrix products, arithmetic and copies ran while one was open for 4% of the time, Pallas kernels for 0%

commit v1 on v0

v1 whole, which is shorter than its diff:
```python
import functools

import jax
import jax.numpy as jnp
from jax import lax
from jax.experimental import pallas as pl
from jax.experimental.pallas import tpu as pltpu
from jax.sharding import PartitionSpec as P

QH = 64
KVH = 8
HD = 128
PER = QH // KVH
DOCS = 16
MESH = pl.DeviceIdType.MESH
BF = jnp.bfloat16
F32 = jnp.float32

UNIT = 256
BLK = 64
BACK = 4
PRE = 1024
KEYS = PRE + (BACK + 1) * UNIT
GROUPS = 2
QCOL = GROUPS * PER * HD
KCOL = GROUPS * HD

ROWS = 128
KC = 256
NCH = KEYS // KC
LANES = PER * ROWS
SCALE = HD ** (-0.5)
LOG2E = 1.4426950408889634


def attention_kernel(
    lens, share, q_ref, do_ref, kv_ref, out_ref, dq_ref, g_ref,
    s_scr, p_scr, q_scr, dot_scr, kt_scr, vt_scr, gk_scr, gv_scr, acc_scr, m_scr, l_scr,
):
    ctx = lax.axis_index("ctx")
    first = ctx * UNIT
    base = first - BACK * UNIT - PRE

    for i in range(NCH):
        kt_scr[i] = kv_ref[0, i * KC:(i + 1) * KC, :].astype(F32).T.astype(BF)
        vt_scr[i] = kv_ref[1, i * KC:(i + 1) * KC, :].astype(F32).T.astype(BF)
    gk_scr[...] = jnp.zeros_like(gk_scr)
    gv_scr[...] = jnp.zeros_like(gv_scr)

    len0 = lens[0]

    def row_block(r, carry):
        p0 = first + r * ROWS
        row_at = pl.multiple_of(r * ROWS, ROWS)
        end = jnp.int32(0)
        own = jnp.int32(0)
        last = jnp.int32(0)
        reads = jnp.int32(0)
        pos = p0 + lax.broadcasted_iota(jnp.int32, (1, LANES), 1) % ROWS
        start_i = jnp.zeros((1, LANES), jnp.int32)
        share_i = jnp.zeros((1, LANES), jnp.int32)
        for d in range(DOCS):
            begin = end
            end = begin + lens[d]
            own = jnp.where(p0 >= begin, begin, own)
            last = jnp.where(p0 + ROWS - 1 >= begin, begin, last)
            inside = pos >= begin
            start_i = jnp.where(inside, begin, start_i)
            if d > 0:
                share_i = jnp.where(inside, share[d], share_i)
                touch = (begin < p0 + ROWS) & (end > p0) & (share[d] == 1)
                reads = jnp.where(touch, jnp.int32(1), reads)
        plim_i = jnp.where(share_i == 1, len0, 0)
        n_pre = jnp.where(reads == 1, (len0 + KC - 1) // KC, 0)
        w_lo = (own - base) // KC
        w_hi = (p0 + ROWS - 1 - base) // KC
        total = n_pre + w_hi - w_lo + 1
        wstart_i = start_i - base
        wend_i = pos - base
        full_lo = last - base
        full_hi = p0 - base

        for h in range(PER):
            q_scr[h * ROWS:(h + 1) * ROWS, :] = q_ref[pl.ds(row_at, ROWS), h * HD:(h + 1) * HD]
        m_scr[...] = jnp.full_like(m_scr, -1e30)
        l_scr[...] = jnp.zeros_like(l_scr)

        def chunk_of(t):
            return jnp.where(t < n_pre, t, t - n_pre + w_lo)

        def score_step(t, carry):
            i = chunk_of(t)
            at = pl.multiple_of(i * KC, KC)
            in_pre = t < n_pre
            s = lax.dot_general(
                kv_ref[0, pl.ds(at, KC), :], q_scr[...], (((1,), (1,)), ((), ())),
                preferred_element_type=F32,
            )
            whole = (i * KC >= full_lo) & (i * KC + KC - 1 <= full_hi) & jnp.logical_not(in_pre)

            @pl.when(whole)
            def _():
                s_scr[pl.ds(at, KC), :] = s
                m_scr[...] = jnp.maximum(m_scr[...], jnp.max(s.reshape(KC // 8, 8, LANES), axis=0))

            @pl.when(jnp.logical_not(whole))
            def _():
                j = i * KC + lax.broadcasted_iota(jnp.int32, (KC, LANES), 0)
                lo = jnp.where(in_pre, 0, wstart_i)
                hi = jnp.where(in_pre, plim_i - 1, wend_i)
                sm = jnp.where((j >= lo) & (j <= hi), s, -1e30)
                s_scr[pl.ds(at, KC), :] = sm
                m_scr[...] = jnp.maximum(m_scr[...], jnp.max(sm.reshape(KC // 8, 8, LANES), axis=0))

            return carry

        lax.fori_loop(0, total, score_step, 0)
        mc = jnp.max(m_scr[...], axis=0, keepdims=True) * (SCALE * LOG2E)
        acc_scr[...] = jnp.zeros_like(acc_scr)

        def value_step(t, carry):
            i = chunk_of(t)
            at = pl.multiple_of(i * KC, KC)
            p = jnp.exp2(s_scr[pl.ds(at, KC), :] * (SCALE * LOG2E) - mc)
            l_scr[...] += jnp.sum(p.reshape(KC // 8, 8, LANES), axis=0)
            pb = p.astype(BF)
            p_scr[pl.ds(at, KC), :] = pb
            acc_scr[...] += jnp.dot(vt_scr[i], pb, preferred_element_type=F32)
            return carry

        lax.fori_loop(0, total, value_step, 0)
        inv = 1.0 / jnp.sum(l_scr[...], axis=0, keepdims=True)
        out_t = acc_scr[...] * inv
        out = out_t.T.astype(BF)
        do_parts = []
        for h in range(PER):
            out_ref[pl.ds(row_at, ROWS), h * HD:(h + 1) * HD] = out[h * ROWS:(h + 1) * ROWS, :]
            do_parts.append(
                do_ref[pl.ds(row_at, ROWS), h * HD:(h + 1) * HD].astype(F32).T
            )
        do_t = (jnp.concatenate(do_parts, axis=1) * inv).astype(BF)
        dot_scr[...] = do_t
        delta = jnp.sum(do_t.astype(F32) * out_t.astype(BF).astype(F32), axis=0, keepdims=True)
        acc_scr[...] = jnp.zeros_like(acc_scr)

        def back_step(t, carry):
            i = chunk_of(t)
            at = pl.multiple_of(i * KC, KC)
            dp = jnp.dot(kv_ref[1, pl.ds(at, KC), :], dot_scr[...], preferred_element_type=F32)
            pb = p_scr[pl.ds(at, KC), :]
            ds = (pb.astype(F32) * (dp - delta)).astype(BF)
            gv_scr[pl.ds(at, KC), :] += lax.dot_general(
                pb, dot_scr[...], (((1,), (1,)), ((), ())), preferred_element_type=F32
            )
            gk_scr[pl.ds(at, KC), :] += jnp.dot(ds, q_scr[...], preferred_element_type=F32)
            acc_scr[...] += jnp.dot(kt_scr[i], ds, preferred_element_type=F32)
            return carry

        lax.fori_loop(0, total, back_step, 0)
        dq = (acc_scr[...] * SCALE).T.astype(BF)
        for h in range(PER):
            dq_ref[pl.ds(row_at, ROWS), h * HD:(h + 1) * HD] = dq[h * ROWS:(h + 1) * ROWS, :]
        return carry

    lax.fori_loop(0, UNIT // ROWS, row_block, 0)
    g_ref[0] = (gk_scr[...] * SCALE).astype(BF)
    g_ref[1] = gv_scr[...].astype(BF)


def attention(q, do, kv, lens, share):
    wide = pl.BlockSpec((UNIT, PER * HD), lambda g: (0, g))
    keys = pl.BlockSpec((2, KEYS, HD), lambda g: (0, 0, g))
    smem = pl.BlockSpec(memory_space=pltpu.SMEM)
    return pl.pallas_call(
        attention_kernel,
        grid=(GROUPS,),
        in_specs=[smem, smem, wide, wide, keys],
        out_specs=[wide, wide, keys],
        out_shape=[
            jax.ShapeDtypeStruct((UNIT, QCOL), BF),
            jax.ShapeDtypeStruct((UNIT, QCOL), BF),
            jax.ShapeDtypeStruct((2, KEYS, KCOL), BF),
        ],
        scratch_shapes=[
            pltpu.VMEM((KEYS, LANES), F32),
            pltpu.VMEM((KEYS, LANES), BF),
            pltpu.VMEM((LANES, HD), BF),
            pltpu.VMEM((HD, LANES), BF),
            pltpu.VMEM((NCH, HD, KC), BF),
            pltpu.VMEM((NCH, HD, KC), BF),
            pltpu.VMEM((KEYS, HD), F32),
            pltpu.VMEM((KEYS, HD), F32),
            pltpu.VMEM((HD, LANES), F32),
            pltpu.VMEM((8, LANES), F32),
            pltpu.VMEM((8, LANES), F32),
        ],
        compiler_params=pltpu.CompilerParams(vmem_limit_bytes=56 * 1024 * 1024),
        name="attention",
    )(lens, share, q, do, kv)


def place():
    ctx = lax.axis_index("ctx")
    y = lax.axis_index("heads")
    core = ctx % 2
    slab = ctx // 2
    return ctx, y, core, slab, slab // 4, slab % 4


def device(slab, core, y):
    return {"ctx": slab * 2 + core, "heads": y}


def gather_kernel(
    q_ref, do_ref, k_ref, v_ref, qg_ref, dog_ref, kv_ref,
    send, recv_q, recv_kv, recv_win, recv_core, recv_piece, recv_x, recv_z, local,
):
    ctx, y, core, slab, z, x = place()
    sibling = device(slab, 1 - core, y)
    barrier = pltpu.get_barrier_semaphore()
    for step in range(1, 4):
        pl.semaphore_signal(barrier, inc=1, device_id=device(slab, core, (y + step) % 4), device_id_type=MESH)
        pl.semaphore_signal(barrier, inc=1, device_id=device(z * 4 + (x + step) % 4, core, y), device_id_type=MESH)
        pl.semaphore_signal(barrier, inc=1, device_id=device((slab + 4 * step) % 16, core, y), device_id_type=MESH)
    for step in (1, 2, 14, 15):
        pl.semaphore_signal(barrier, inc=1, device_id=device((slab + step) % 16, core, y), device_id_type=MESH)
    pl.semaphore_signal(barrier, inc=1, device_id=sibling, device_id_type=MESH)
    source = (z == 0) & (x < 2)
    origin = z // 2

    @pl.when(source)
    def _():
        for i in range(8):
            @pl.when(8 * x + i != slab)
            def _():
                pl.semaphore_signal(barrier, inc=1, device_id=device(8 * x + i, core, y), device_id_type=MESH)

    @pl.when(slab != origin)
    def _():
        pl.semaphore_signal(barrier, inc=1, device_id=device(origin, core, y), device_id_type=MESH)

    pl.semaphore_wait(barrier, 14 + jnp.where(slab == 0, 7, jnp.where(slab == 1, 9, 1)))

    own = PRE + BACK * UNIT
    mine = pl.multiple_of(y * BLK, BLK)

    copies = []
    here = []
    for n, ref in enumerate((k_ref, v_ref)):
        for step in range(1, 4):
            to = (y + step) % 4
            col = pl.multiple_of(to * KCOL, KCOL)
            copy = pltpu.make_async_remote_copy(
                src_ref=ref.at[:, pl.ds(col, KCOL)],
                dst_ref=kv_ref.at[n, pl.ds(own + mine, BLK), :],
                send_sem=send.at[n * 3 + step - 1],
                recv_sem=recv_kv.at[n * 3 + step - 1],
                device_id=device(slab, core, to),
                device_id_type=MESH,
            )
            copy.start()
            copies.append(copy)
        col = pl.multiple_of(y * KCOL, KCOL)
        copy = pltpu.make_async_copy(
            ref.at[:, pl.ds(col, KCOL)], kv_ref.at[n, pl.ds(own + mine, BLK), :], local.at[n]
        )
        copy.start()
        here.append(copy)
    kv_copies = copies
    q_copies = []
    for n, (ref, out) in enumerate(((q_ref, qg_ref), (do_ref, dog_ref))):
        for step in range(1, 4):
            to = (y + step) % 4
            col = pl.multiple_of(to * QCOL, QCOL)
            copy = pltpu.make_async_remote_copy(
                src_ref=ref.at[:, pl.ds(col, QCOL)],
                dst_ref=out.at[pl.ds(mine, BLK), :],
                send_sem=send.at[6 + n * 3 + step - 1],
                recv_sem=recv_q.at[n * 3 + step - 1],
                device_id=device(slab, core, to),
                device_id_type=MESH,
            )
            copy.start()
            q_copies.append(copy)
        col = pl.multiple_of(y * QCOL, QCOL)
        copy = pltpu.make_async_copy(
            ref.at[:, pl.ds(col, QCOL)], out.at[pl.ds(mine, BLK), :], local.at[2 + n]
        )
        copy.start()
        here.append(copy)
    here[0].wait()
    here[1].wait()
    for copy in kv_copies:
        copy.wait_recv()

    def rows(at, count):
        return kv_ref.at[:, pl.ds(at, count), :]

    def send_rows(src, dst, count, send_sem, recv_sem, to):
        return pltpu.make_async_remote_copy(
            src_ref=rows(src, count), dst_ref=rows(dst, count), send_sem=send_sem,
            recv_sem=recv_sem, device_id=to, device_id_type=MESH,
        )

    slot = [PRE + i * UNIT for i in range(BACK + 1)]
    part = 32
    piece = (core + 2 * origin) * UNIT + (slab % 8) * part
    piece = pl.multiple_of(piece, part)

    def scatter(i):
        return send_rows(
            pl.multiple_of(own + i * part, part),
            pl.multiple_of((core + 2 * x) * UNIT + i * part, part),
            part, send.at[12 + i], recv_piece, device(8 * x + i, core, y),
        )

    own_piece = pltpu.make_async_copy(
        rows(own, part), rows(pl.multiple_of(core * UNIT, part), part), local.at[4]
    )

    @pl.when(source)
    def _():
        for i in range(8):
            @pl.when(8 * x + i != slab)
            def _():
                scatter(i).start()

    @pl.when(slab == 0)
    def _():
        own_piece.start()

    def window(ahead):
        return send_rows(
            own, slot[2] if ahead == 1 else slot[0], UNIT, send.at[20 + ahead], recv_win.at[ahead - 1],
            device((slab + ahead) % 16, core, y),
        )

    for ahead in (1, 2):
        @pl.when(slab + ahead < 16)
        def _():
            window(ahead).start()

    core_own = send_rows(own, slot[3], UNIT, send.at[23], recv_core.at[0], sibling)

    @pl.when(core == 0)
    def _():
        core_own.start()

    @pl.when(slab == 0)
    def _():
        own_piece.wait()

    @pl.when(slab != 0)
    def _():
        send_rows(piece, piece, part, send.at[12], recv_piece, sibling).wait_recv()

    x_copies = []
    for step in range(1, 4):
        copy = send_rows(
            piece, piece, part, send.at[24 + step - 1], recv_x.at[step - 1],
            device(z * 4 + (x + step) % 4, core, y),
        )
        copy.start()
        x_copies.append(copy)
    for copy in x_copies:
        copy.wait_recv()
    plane = pl.multiple_of((core + 2 * origin) * UNIT + (z % 2) * 4 * part, 4 * part)
    z_copies = []
    for step in range(1, 4):
        copy = send_rows(
            plane, plane, 4 * part, send.at[27 + step - 1], recv_z.at[step - 1],
            device((slab + 4 * step) % 16, core, y),
        )
        copy.start()
        z_copies.append(copy)
    pass_near = [
        send_rows(slot[2], slot[1], UNIT, send.at[30], recv_core.at[1], sibling),
        send_rows(slot[2], slot[3], UNIT, send.at[30], recv_core.at[0], sibling),
    ]
    pass_far = send_rows(slot[0], slot[1], UNIT, send.at[31], recv_core.at[1], sibling)

    @pl.when(slab >= 1)
    def _():
        window(1).wait_recv()

        @pl.when(core == 0)
        def _():
            pass_near[0].start()

        @pl.when(core == 1)
        def _():
            pass_near[1].start()

    @pl.when(slab >= 2)
    def _():
        window(2).wait_recv()

        @pl.when(core == 1)
        def _():
            pass_far.start()

    for copy in z_copies:
        copy.wait_recv()
    halves = []
    for i in range(2):
        at = pl.multiple_of((core + 2 * i) * UNIT, UNIT)
        copy = send_rows(at, at, UNIT, send.at[32 + i], recv_core.at[2 + i], sibling)
        copy.start()
        halves.append(copy)

    for copy in q_copies:
        copy.wait_recv()
    here[2].wait()
    here[3].wait()
    for copy in halves:
        copy.wait_recv()

    @pl.when(core == 1)
    def _():
        core_own.wait_recv()

        @pl.when(slab >= 1)
        def _():
            pass_near[0].wait_recv()

    @pl.when(core == 0)
    def _():
        @pl.when(slab >= 1)
        def _():
            pass_near[1].wait_recv()

        @pl.when(slab >= 2)
        def _():
            pass_far.wait_recv()

    for copy in kv_copies + q_copies + x_copies + z_copies + halves:
        copy.wait_send()

    @pl.when(source)
    def _():
        for i in range(8):
            @pl.when(8 * x + i != slab)
            def _():
                scatter(i).wait_send()

    for ahead in (1, 2):
        @pl.when(slab + ahead < 16)
        def _():
            window(ahead).wait_send()

    @pl.when(core == 0)
    def _():
        core_own.wait_send()

    @pl.when(slab >= 1)
    def _():
        pass_near[0].wait_send()

    @pl.when((slab >= 2) & (core == 1))
    def _():
        pass_far.wait_send()


def gather(q, do, k, v):
    any_spec = pl.BlockSpec(memory_space=pl.ANY)
    return pl.pallas_call(
        gather_kernel,
        in_specs=[any_spec] * 4,
        out_specs=[any_spec] * 3,
        out_shape=[
            jax.ShapeDtypeStruct((UNIT, QCOL), BF),
            jax.ShapeDtypeStruct((UNIT, QCOL), BF),
            jax.ShapeDtypeStruct((2, KEYS, KCOL), BF),
        ],
        scratch_shapes=[
            pltpu.SemaphoreType.DMA((34,)),
            pltpu.SemaphoreType.DMA((6,)),
            pltpu.SemaphoreType.DMA((6,)),
            pltpu.SemaphoreType.DMA((2,)),
            pltpu.SemaphoreType.DMA((4,)),
            pltpu.SemaphoreType.DMA,
            pltpu.SemaphoreType.DMA((3,)),
            pltpu.SemaphoreType.DMA((3,)),
            pltpu.SemaphoreType.DMA((5,)),
        ],
        compiler_params=pltpu.CompilerParams(collective_id=0, has_side_effects=True),
        name="gather",
    )(q, do, k, v)


def reduce_kernel(
    out_ref, dq_ref, g_ref, o_ref, odq_ref, dk_ref, dv_ref,
    own_buf, core_buf, z_send, z_buf, x_send, x_buf, last_send, last_buf, w_send, w_buf, sum_buf, k_buf,
    send, recv_q, recv_core, recv_z, recv_x, recv_last, recv_win, recv_k, local,
):
    ctx, y, core, slab, z, x = place()
    sibling = device(slab, 1 - core, y)
    barrier = pltpu.get_barrier_semaphore()
    for step in range(1, 4):
        pl.semaphore_signal(barrier, inc=1, device_id=device(slab, core, (y + step) % 4), device_id_type=MESH)
        pl.semaphore_signal(barrier, inc=1, device_id=device(z * 4 + (x + step) % 4, core, y), device_id_type=MESH)
        pl.semaphore_signal(barrier, inc=1, device_id=device((slab + 4 * step) % 16, core, y), device_id_type=MESH)
    for step in (1, 2, 14, 15):
        pl.semaphore_signal(barrier, inc=1, device_id=device((slab + step) % 16, core, y), device_id_type=MESH)
    pl.semaphore_signal(barrier, inc=1, device_id=sibling, device_id_type=MESH)
    source = (z == 0) & (x < 2)
    origin = z // 2

    @pl.when(source)
    def _():
        for i in range(8):
            @pl.when(8 * x + i != slab)
            def _():
                pl.semaphore_signal(barrier, inc=1, device_id=device(8 * x + i, core, y), device_id_type=MESH)

    @pl.when(slab != origin)
    def _():
        pl.semaphore_signal(barrier, inc=1, device_id=device(origin, core, y), device_id_type=MESH)

    pl.semaphore_wait(barrier, 14 + jnp.where(slab == 0, 7, jnp.where(slab == 1, 9, 1)))

    mine = pl.multiple_of(y * BLK, BLK)

    def g_rows(at, count):
        return g_ref.at[:, pl.ds(at, count), :]

    def remote(src, dst, send_sem, recv_sem, to):
        return pltpu.make_async_remote_copy(
            src_ref=src, dst_ref=dst, send_sem=send_sem, recv_sem=recv_sem,
            device_id=to, device_id_type=MESH,
        )

    core_copies = []
    for i in range(2):
        at = pl.multiple_of((1 - core + 2 * i) * UNIT, UNIT)
        copy = remote(g_rows(at, UNIT), core_buf.at[i], send.at[i], recv_core.at[i], sibling)
        copy.start()
        core_copies.append(copy)
    for i in range(2):
        copy = remote(
            g_rows(PRE + (1 + 2 * i) * UNIT, UNIT), core_buf.at[2 + i], send.at[2 + i], recv_core.at[2 + i], sibling
        )
        copy.start()
        core_copies.append(copy)
    loads = []
    for i in range(2):
        at = pl.multiple_of((core + 2 * i) * UNIT, UNIT)
        copy = pltpu.make_async_copy(g_rows(at, UNIT), own_buf.at[i], local.at[i])
        copy.start()
        loads.append(copy)
    for i in range(3):
        copy = pltpu.make_async_copy(g_rows(PRE + 2 * i * UNIT, UNIT), own_buf.at[2 + i], local.at[2 + i])
        copy.start()
        loads.append(copy)

    q_copies = []
    here = []
    for n, (ref, out) in enumerate(((out_ref, o_ref), (dq_ref, odq_ref))):
        for step in range(1, 4):
            to = (y + step) % 4
            col = pl.multiple_of(y * QCOL, QCOL)
            copy = remote(
                ref.at[pl.ds(pl.multiple_of(to * BLK, BLK), BLK), :],
                out.at[:, pl.ds(col, QCOL)],
                send.at[4 + n * 3 + step - 1], recv_q.at[n * 3 + step - 1], device(slab, core, to),
            )
            copy.start()
            q_copies.append(copy)
        copy = pltpu.make_async_copy(
            ref.at[pl.ds(mine, BLK), :],
            out.at[:, pl.ds(pl.multiple_of(y * QCOL, QCOL), QCOL)],
            local.at[5 + n],
        )
        copy.start()
        here.append(copy)

    part = 32
    for i in range(2):
        loads[i].wait()
        core_copies[i].wait_recv()
        z_send[i] = (own_buf[i].astype(F32) + core_buf[i].astype(F32)).astype(BF)
    z_copies = []
    for step in range(1, 4):
        to = (z + step) % 4
        at = pl.multiple_of((to % 2) * 4 * part, 4 * part)
        copy = remote(
            z_send.at[to // 2, :, pl.ds(at, 4 * part), :], z_buf.at[step - 1],
            send.at[10 + step - 1], recv_z.at[step - 1], device((slab + 4 * step) % 16, core, y),
        )
        copy.start()
        z_copies.append(copy)

    for i in range(3):
        loads[2 + i].wait()
    core_copies[2].wait_recv()
    core_copies[3].wait_recv()
    a = core_buf[2].astype(F32)
    b = core_buf[3].astype(F32)
    lower = core == 0
    far = own_buf[2].astype(F32)
    near = own_buf[3].astype(F32)
    w_send[0] = (near + jnp.where(lower, a, b)).astype(BF)
    w_send[1] = jnp.where(lower, far, far + a).astype(BF)
    sum_buf[...] = own_buf[4].astype(F32) + jnp.where(lower, b, 0.0)

    def window(back):
        return remote(
            w_send.at[back - 1], w_buf.at[back - 1], send.at[13 + back], recv_win.at[back - 1],
            device((slab + 16 - back) % 16, core, y),
        )

    for back in (1, 2):
        @pl.when(slab >= back)
        def _():
            window(back).start()

    for copy in z_copies:
        copy.wait_recv()
    at = pl.multiple_of((z % 2) * 4 * part, 4 * part)
    total = z_send[z // 2, :, pl.ds(at, 4 * part), :].astype(F32)
    for i in range(3):
        total += z_buf[i].astype(F32)
    x_send[...] = total.astype(BF)
    x_copies = []
    for step in range(1, 4):
        to = (x + step) % 4
        copy = remote(
            x_send.at[:, pl.ds(pl.multiple_of(to * part, part), part), :], x_buf.at[step - 1],
            send.at[16 + step - 1], recv_x.at[step - 1], device(z * 4 + to, core, y),
        )
        copy.start()
        x_copies.append(copy)
    for copy in x_copies:
        copy.wait_recv()
    total = x_send[:, pl.ds(pl.multiple_of(x * part, part), part), :].astype(F32)
    for i in range(3):
        total += x_buf[i].astype(F32)
    last_send[...] = total.astype(BF)

    at = pl.multiple_of((slab % 8) * part, part)
    home = remote(last_send, last_buf.at[:, pl.ds(at, part), :], send.at[19], recv_last.at[slab % 8], device(origin, core, y))

    def arrival(i):
        return remote(last_send, last_buf.at[:, pl.ds(i * part, part), :], send.at[19], recv_last.at[i], sibling)

    @pl.when(slab != origin)
    def _():
        home.start()

    for back in (1, 2):
        @pl.when(slab + back < 16)
        def _():
            window(back).wait_recv()
            sum_buf[...] += w_buf[back - 1].astype(F32)

    @pl.when(source)
    def _():
        for i in range(8):
            @pl.when(8 * x + i != slab)
            def _():
                arrival(i).wait_recv()

        @pl.when(slab == 0)
        def _():
            last_buf[:, 0:part, :] = last_send[...]

        sum_buf[...] += last_buf[...].astype(F32)

    k_buf[...] = sum_buf[...].astype(BF)
    k_copies = []
    col = pl.multiple_of(y * KCOL, KCOL)
    for n, out in enumerate((dk_ref, dv_ref)):
        for step in range(1, 4):
            to = (y + step) % 4
            copy = remote(
                k_buf.at[n, pl.ds(pl.multiple_of(to * BLK, BLK), BLK), :], out.at[:, pl.ds(col, KCOL)],
                send.at[20 + n * 3 + step - 1], recv_k.at[n * 3 + step - 1], device(slab, core, to),
            )
            copy.start()
            k_copies.append(copy)
        copy = pltpu.make_async_copy(k_buf.at[n, pl.ds(mine, BLK), :], out.at[:, pl.ds(col, KCOL)], local.at[7 + n])
        copy.start()
        here.append(copy)

    for copy in here:
        copy.wait()
    for copy in q_copies + k_copies:
        copy.wait_recv()
    for copy in core_copies + q_copies + z_copies + x_copies + k_copies:
        copy.wait_send()

    @pl.when(slab != origin)
    def _():
        home.wait_send()

    for back in (1, 2):
        @pl.when(slab >= back)
        def _():
            window(back).wait_send()


def reduce(out, dq, g):
    any_spec = pl.BlockSpec(memory_space=pl.ANY)
    unit = (2, UNIT, KCOL)
    return pl.pallas_call(
        reduce_kernel,
        in_specs=[any_spec] * 3,
        out_specs=[any_spec] * 4,
        out_shape=[
            jax.ShapeDtypeStruct((BLK, QH * HD), BF),
            jax.ShapeDtypeStruct((BLK, QH * HD), BF),
            jax.ShapeDtypeStruct((BLK, KVH * HD), BF),
            jax.ShapeDtypeStruct((BLK, KVH * HD), BF),
        ],
        scratch_shapes=[
            pltpu.VMEM((5,) + unit, BF),
            pltpu.VMEM((4,) + unit, BF),
            pltpu.VMEM((2,) + unit, BF),
            pltpu.VMEM((3, 2, 128, KCOL), BF),
            pltpu.VMEM((2, 128, KCOL), BF),
            pltpu.VMEM((3, 2, 32, KCOL), BF),
            pltpu.VMEM((2, 32, KCOL), BF),
            pltpu.VMEM(unit, BF),
            pltpu.VMEM((2,) + unit, BF),
            pltpu.VMEM((2,) + unit, BF),
            pltpu.VMEM(unit, F32),
            pltpu.VMEM(unit, BF),
            pltpu.SemaphoreType.DMA((26,)),
            pltpu.SemaphoreType.DMA((6,)),
            pltpu.SemaphoreType.DMA((4,)),
            pltpu.SemaphoreType.DMA((3,)),
            pltpu.SemaphoreType.DMA((3,)),
            pltpu.SemaphoreType.DMA((8,)),
            pltpu.SemaphoreType.DMA((2,)),
            pltpu.SemaphoreType.DMA((6,)),
            pltpu.SemaphoreType.DMA((9,)),
        ],
        compiler_params=pltpu.CompilerParams(
            collective_id=1, has_side_effects=True, vmem_limit_bytes=32 * 1024 * 1024
        ),
        name="reduce",
    )(out, dq, g)


def on_device(queries, keys, values, grad_out, doc_lengths, share_prefix):
    q, do, kv = gather(queries, grad_out, keys, values)
    out, dq, g = attention(q, do, kv, doc_lengths, share_prefix)
    return tuple(reduce(out, dq, g))


def solution(mesh):
    rows = P(("ctx", "heads"), None)
    return jax.shard_map(
        on_device, mesh=mesh, in_specs=(rows, rows, rows, rows, P(), P()),
        out_specs=(rows, rows, rows, rows), check_vma=False,
    )
```

time: 619 us -> 131 us (0.21); the launches traced: 626 us -> 131 us
  waiting for transfers between devices: 298 us -> 0 us
  local copies, waits for them, and re-layouts: 168 us -> 7.36 us
  Pallas kernels: 0 us -> 123 us
  other arithmetic: 45.5 us -> 0 us
  matrix products: 35.4 us -> 0 us
  starting transfers between devices: 24.3 us -> 0 us
  loops' own time: 21.2 us -> 0 us
  blocking collectives: 19.4 us -> 0 us
  between operations: 13.9 us -> 0.65 us
    reduce_scatter x2 -> x0, waiting for transfers between devices: 221 us -> none  [the longest x1 130 us: on_device(): lax.psum_scatter(k_terms, 'ctx', scatter_dimension=0, tiled=True)]
    pallas_call x0 -> x3, Pallas kernels: none -> 123 us  [the longest x1 60.1 us: reduce(): pl.pallas_call(reduce_kernel, in_specs=[any_spec] * 3, out_specs=[any_spe...]
    dynamic_update_slice x48 -> x0, local copies, waits for them, and re-layouts: 102 us -> none  [on_device(): lax.scan(back_step, jnp.zeros((tok, groups, per, HD), jnp.float32), (k_st...]
    all_gather x2 -> x0, waiting for transfers between devices: 40.4 us -> none  [the longest x1 40.4 us: on_device(): lax.all_gather(v_loc, 'ctx', axis=0, tiled=True)]
    all_to_all x6 -> x0, waiting for transfers between devices: 36.8 us -> none  [the longest x1 13.4 us: on_device(): lax.all_to_all(out_rows, 'heads', split_axis=0, concat_axis=1, tiled=True)]
    dot_general x14 -> x0, matrix products: 35.4 us -> none  [the longest x2 6.96 us: back_compute(): jnp.einsum('gjts,tgjd->sgd', prob.astype(jnp.bfloat16), do_four, preferre...]
    reduce_or x32 -> x0, other arithmetic: 30.1 us -> none  [the longest x16 15.5 us: back_step(): return lax.cond(jnp.any(allowed), back_compute, passby, grad_q)]
    broadcast_in_dim x30 -> x0, local copies, waits for them, and re-layouts: 24.6 us -> none  [the longest x28 24.6 us: on_device(): lax.scan(back_step, jnp.zeros((tok, groups, per, HD), jnp.float32), (k_st...]
  transfers between devices with their start and end apart: 10 -> 0, of which waited for: 7 -> 0; matrix products, arithmetic and copies ran while one was open for 4% -> 0% of each run, Pallas kernels for 0% -> 0%
where the time goes in v1:
time: 131 us
  Pallas kernels  123 us (94%)
  local copies, waits for them, and re-layouts  7.36 us (6%)
    pallas_call x1, Pallas kernels, reduce(): pl.pallas_call(reduce_kernel, in_specs=[any_spec] * 3, out_specs=[any_spe...  60.1 us
    pallas_call x1, Pallas kernels, gather(): pl.pallas_call(gather_kernel, in_specs=[any_spec] * 4, out_specs=[any_spe...  39.1 us
    pallas_call x1, Pallas kernels, attention(): pl.pallas_call(attention_kernel, grid=(GROUPS,), in_specs=[smem, smem, wi...  23.8 us
    unnamed x10, local copies, waits for them, and re-layouts  7.36 us

profile of v1, /device:TPU:2, one launch (start us, length us, event | category | flops | bytes accessed | tf_op | source)
XLA Modules:
  0.0 130.9 jit_solution(18411735175984967919)
XLA Ops:
  0.6 39.1 %gather.1 = (bf16[256,2048]{1,0:T(8,128)(2,1)}, bf16[256,2048]{1,0:T(8,128)(2,1)}, bf16[2,2304,256]{2,1,0:T(8,128)(2,1)}) custom-call(bf16[64,8192]{1,0:T(8,128)(2,1)} %q_ref.1, bf16[64,8192]{1,0:T(8,128)(2,1)} %do_ref.1, bf16[64,1024]{1,0:T(8,128)(2,1)} %k_ref.1, bf16[64,1024]{1,0:T(8,128)(2,1)} %v_ref.1), custom_call_target="tpu_custom_call" | custom-call | tf_op jit(solution)/shard_map/gather/pallas_call | solution.py:466
  39.7 23.8 %attention.1 = (bf16[256,2048]{1,0:T(8,128)(2,1)}, bf16[256,2048]{1,0:T(8,128)(2,1)}, bf16[2,2304,256]{2,1,0:T(8,128)(2,1)}) custom-call(s32[16]{0:T(128)} %lens.1, s32[16]{0:T(128)} %share.1, bf16[256,2048]{1,0:T(8,128)(2,1)} %get-tuple-element.10.q_ref, bf16[256,2048]{1,0:T(8,128)(2,1)} %get-tuple-element.11.do_ref, ...), custom_call_target="tpu_custom_call" | custom-call | tf_op jit(solution)/shard_map/attention/pallas_call | solution.py:174
  63.5 0.0 copy-start
  63.5 1.7 %copy-done = bf16[2,2304,256]{2,1,0:T(8,128)(2,1)S(1)} copy-done((bf16[2,2304,256]{2,1,0:T(8,128)(2,1)S(1)}, bf16[2,2304,256]{2,1,0:T(8,128)(2,1)}, u32[]{:S(2)}) %copy-start) | copy-done | bytes 2359320
  65.2 0.0 copy-start.1
  65.2 1.2 copy-done.1
  66.4 0.0 copy-start.2
  66.4 1.2 copy-done.2
  67.6 60.1 %reduce.1 = (bf16[64,8192]{1,0:T(8,128)(2,1)S(1)}, bf16[64,8192]{1,0:T(8,128)(2,1)S(1)}, bf16[64,1024]{1,0:T(8,128)(2,1)S(1)}, bf16[64,1024]{1,0:T(8,128)(2,1)S(1)}) custom-call(bf16[256,2048]{1,0:T(8,128)(2,1)S(1)} %copy-done.1, bf16[256,2048]{1,0:T(8,128)(2,1)S(1)} %copy-done.2, bf16[2,2304,256]{2,1,0:T(8,128)(2,1)S(1)} %copy-done), custom_call_target="tpu_custom_call" | custom-call | tf_op jit(solution)/shard_map/reduce/pallas_call | solution.py:705
  127.7 1.0 copy.14
  128.7 1.0 copy.15
  129.6 0.7 copy.16
  130.3 0.7 copy.17
Async XLA Ops:
  63.5 1.7 %copy-start = (bf16[2,2304,256]{2,1,0:T(8,128)(2,1)S(1)}, bf16[2,2304,256]{2,1,0:T(8,128)(2,1)}, u32[]{:S(2)}) copy-start(bf16[2,2304,256]{2,1,0:T(8,128)(2,1)} %get-tuple-element.15.g_ref) | copy-start | bytes 7077892
  65.2 1.2 copy-start.1
  66.4 1.2 copy-start.2

commit v2 on v0

v2 whole, which is shorter than its diff:
```python
import jax
import jax.numpy as jnp
from jax import lax
from jax.experimental import pallas as pl
from jax.experimental.pallas import tpu as pltpu
from jax.sharding import PartitionSpec as P

QH = 64
KVH = 8
HD = 128
PER = QH // KVH
DOCS = 16
MESH = pl.DeviceIdType.MESH
BF = jnp.bfloat16
F32 = jnp.float32

UNIT = 256
BLK = 64
BACK = 4
PRE = 1024
KEYS = PRE + (BACK + 1) * UNIT
GROUPS = 2
WIDE = PER * HD

ROWS = 128
LANES = PER * ROWS
SEEN = PRE + BACK * UNIT + ROWS
KC = 512
SCALE = HD ** (-0.5)
LOG2E = 1.4426950408889634
PART = 32
SEMS = 192
NT = (((1,), (1,)), ((), ()))


def kernel(
    lens, share, q_ref, do_ref, k_ref, v_ref, o_ref, odq_ref, dk_ref, dv_ref,
    q_in, do_in, kv, kt, s_scr, p_scr, q_scr, dot_scr, acc, m_scr, l_scr, gk, gv, out_buf, dq_buf,
    g_buf, core_buf, z_send, z_buf, x_send, x_buf, last_send, last_buf, w_send, w_buf, sum_buf, k_buf,
    send, recv, local,
):
    ctx = lax.axis_index("ctx")
    y = lax.axis_index("heads")
    core = ctx % 2
    slab = ctx // 2
    z = slab // 4
    x = slab % 4
    origin = z // 2
    source = (z == 0) & (x < 2)
    mine = pl.multiple_of(y * BLK, BLK)
    own = PRE + BACK * UNIT
    slot = [PRE + i * UNIT for i in range(BACK + 1)]

    def device(to_slab, to_core, to_y):
        return {"ctx": to_slab * 2 + to_core, "heads": to_y}

    sibling = device(slab, 1 - core, y)
    peers = [(y + 2) % 4, 3 - y, y + 1 - 2 * (y % 2)]

    @pl.when(slab < 2)
    def _():
        for g in range(GROUPS):
            kv[g, :, PRE:own, :] = jnp.zeros((2, BACK * UNIT, HD), BF)

    barrier = pltpu.get_barrier_semaphore()

    def greet(to):
        pl.semaphore_signal(barrier, inc=1, device_id=to, device_id_type=MESH)

    for step in range(1, 4):
        greet(device(slab, core, (y + step) % 4))
        greet(device(z * 4 + (x + step) % 4, core, y))
        greet(device((slab + 4 * step) % 16, core, y))
    for step in (1, 2, 14, 15):
        greet(device((slab + step) % 16, core, y))
    greet(sibling)

    @pl.when(source)
    def _():
        for i in range(8):
            @pl.when(8 * x + i != slab)
            def _():
                greet(device(8 * x + i, core, y))

    @pl.when(slab != origin)
    def _():
        greet(device(origin, core, y))

    pl.semaphore_wait(barrier, 14 + jnp.where(slab == 0, 7, jnp.where(slab == 1, 9, 1)))

    table = {}

    def number(name, count=1):
        if name not in table:
            table[name] = sum(c for _, c in table.values()), count
        return table[name][0]

    def remote(name, src, dst, to, shift=0, sent=None):
        at = number(name, 8 if name[0] == "home" else 1) + shift
        out = at if sent is None else number(sent)
        return pltpu.make_async_remote_copy(
            src_ref=src, dst_ref=dst, send_sem=send.at[out], recv_sem=recv.at[at],
            device_id=to, device_id_type=MESH,
        )


    def kv_head(g, i):
        n, ref = ((0, k_ref), (1, v_ref))[i // 4]
        to = (peers + [y])[i % 4]
        src = ref.at[:, pl.ds(pl.multiple_of((to * GROUPS + g) * HD, HD), HD)]
        dst = kv.at[g, n, pl.ds(own + mine, BLK), :]
        if i % 4 == 3:
            return pltpu.make_async_copy(src, dst, local.at[g * 2 + n])
        return remote(("kv", g, i), src, dst, device(slab, core, to))

    def q_head(g, i, n):
        ref, into = ((q_ref, q_in), (do_ref, do_in))[n]
        to = (peers + [y])[i]
        src = ref.at[:, pl.ds(pl.multiple_of((to * GROUPS + g) * WIDE, WIDE), WIDE)]
        dst = into.at[g, pl.ds(mine, BLK), :]
        if i == 3:
            return pltpu.make_async_copy(src, dst, local.at[4 + g * 2 + n])
        return remote(("q", g, i, n), src, dst, device(slab, core, to))

    def rows(g, at, count):
        return kv.at[g, :, pl.ds(at, count), :]

    def move(name, g, src, dst, count, to, sent=None):
        return remote((name, g), rows(g, src, count), rows(g, dst, count), to, sent=sent)

    piece = pl.multiple_of((core + 2 * origin) * UNIT + (slab % 8) * PART, PART)
    plane = pl.multiple_of((core + 2 * origin) * UNIT + (z % 2) * 4 * PART, 4 * PART)

    def scatter(g, i):
        return move(
            "piece", g, own + i * PART, pl.multiple_of((core + 2 * x) * UNIT + i * PART, PART), PART,
            device(8 * x + i, core, y), sent=("scatter", g, i),
        )

    def own_piece(g):
        return pltpu.make_async_copy(
            rows(g, own, PART), rows(g, pl.multiple_of(core * UNIT, PART), PART), local.at[8 + g]
        )

    def window(g, ahead):
        return move(
            ("window", ahead), g, own, slot[2] if ahead == 1 else slot[0], UNIT,
            device((slab + ahead) % 16, core, y),
        )

    def along_x(g, step):
        return move(("x", step), g, piece, piece, PART, device(z * 4 + (x + step) % 4, core, y))

    def along_z(g, step):
        return move(("z", step), g, plane, plane, 4 * PART, device((slab + 4 * step) % 16, core, y))

    def core_own(g):
        return move(("core", 3), g, own, slot[3], UNIT, sibling)

    def near_up(g):
        return move(("core", 1), g, slot[2], slot[1], UNIT, sibling)

    def near_down(g):
        return move(("core", 3), g, slot[2], slot[3], UNIT, sibling)

    def far_down(g):
        return move(("core", 1), g, slot[0], slot[1], UNIT, sibling)

    def half(g, i):
        at = pl.multiple_of((core + 2 * i) * UNIT, UNIT)
        return move(("half", i), g, at, at, UNIT, sibling)

    def kv_start(g):
        for i in range(8):
            kv_head(g, i).start()

    def q_start(g):
        for i in range(4):
            for n in range(2):
                q_head(g, i, n).start()

    def kv_stage1(g):
        for i in range(8):
            if i % 4 == 3:
                kv_head(g, i).wait()
            else:
                kv_head(g, i).wait_recv()

        @pl.when(source)
        def _():
            for i in range(8):
                @pl.when(8 * x + i != slab)
                def _():
                    scatter(g, i).start()

        @pl.when(slab == 0)
        def _():
            own_piece(g).start()

        for ahead in (1, 2):
            @pl.when(slab + ahead < 16)
            def _():
                window(g, ahead).start()

        @pl.when(core == 0)
        def _():
            core_own(g).start()

    def kv_stage2(g):
        @pl.when(slab == 0)
        def _():
            own_piece(g).wait()

        @pl.when(slab != 0)
        def _():
            move("piece", g, piece, piece, PART, sibling).wait_recv()

        for step in range(1, 4):
            along_x(g, step).start()

    def kv_stage3(g):
        for step in range(1, 4):
            along_x(g, step).wait_recv()
        for step in range(1, 4):
            along_z(g, step).start()

    def kv_stage4(g):
        for step in range(1, 4):
            along_z(g, step).wait_recv()
        for i in range(2):
            half(g, i).start()

    def kv_stage5(g):
        @pl.when(slab >= 1)
        def _():
            window(g, 1).wait_recv()

            @pl.when(core == 0)
            def _():
                near_up(g).start()

            @pl.when(core == 1)
            def _():
                near_down(g).start()

        @pl.when(slab >= 2)
        def _():
            window(g, 2).wait_recv()

            @pl.when(core == 1)
            def _():
                far_down(g).start()

    def kv_stage6(g):
        for i in range(2):
            half(g, i).wait_recv()

        @pl.when(core == 1)
        def _():
            core_own(g).wait_recv()

            @pl.when(slab >= 1)
            def _():
                near_up(g).wait_recv()

        @pl.when(core == 0)
        def _():
            @pl.when(slab >= 1)
            def _():
                near_down(g).wait_recv()

            @pl.when(slab >= 2)
            def _():
                far_down(g).wait_recv()


    def q_back(g, i, n):
        buf, ref = ((out_buf, o_ref), (dq_buf, odq_ref))[n]
        to = (peers + [y])[i]
        src = buf.at[g, pl.ds(pl.multiple_of(to * BLK, BLK), BLK), :]
        dst = ref.at[:, pl.ds(pl.multiple_of((y * GROUPS + g) * WIDE, WIDE), WIDE)]
        if i == 3:
            return pltpu.make_async_copy(src, dst, local.at[10 + g * 2 + n])
        return remote(("back", g, i, n), src, dst, device(slab, core, to))

    def g_rows(g, at, count):
        return g_buf.at[g, :, pl.ds(at, count), :]

    def core_sum(g, i):
        if i < 2:
            at = pl.multiple_of((1 - core + 2 * i) * UNIT, UNIT)
        else:
            at = slot[1 + 2 * (i - 2)]
        return remote(("csum", g, i), g_rows(g, at, UNIT), core_buf.at[g, i], sibling)

    def z_sum(g, step):
        to = (z + step) % 4
        at = pl.multiple_of((to % 2) * 4 * PART, 4 * PART)
        return remote(
            ("zsum", g, step), z_send.at[g, to // 2, :, pl.ds(at, 4 * PART), :], z_buf.at[g, step - 1],
            device((slab + 4 * step) % 16, core, y),
        )

    def x_sum(g, step):
        to = (x + step) % 4
        at = pl.multiple_of(to * PART, PART)
        return remote(
            ("xsum", g, step), x_send.at[g, :, pl.ds(at, PART), :], x_buf.at[g, step - 1],
            device(z * 4 + to, core, y),
        )

    def home(g):
        at = pl.multiple_of((slab % 8) * PART, PART)
        return remote(
            ("home", g), last_send.at[g], last_buf.at[g, :, pl.ds(at, PART), :], device(origin, core, y),
            shift=slab % 8, sent=("went", g),
        )

    def arrival(g, i):
        return remote(
            ("home", g), last_send.at[g], last_buf.at[g, :, pl.ds(i * PART, PART), :], sibling,
            shift=i, sent=("went", g),
        )

    def w_sum(g, back):
        return remote(
            ("wsum", g, back), w_send.at[g, back - 1], w_buf.at[g, back - 1],
            device((slab + 16 - back) % 16, core, y),
        )

    def k_back(g, i, n):
        ref = (dk_ref, dv_ref)[n]
        to = (peers + [y])[i]
        src = k_buf.at[g, n, pl.ds(pl.multiple_of(to * BLK, BLK), BLK), :]
        dst = ref.at[:, pl.ds(pl.multiple_of((y * GROUPS + g) * HD, HD), HD)]
        if i == 3:
            return pltpu.make_async_copy(src, dst, local.at[14 + g * 2 + n])
        return remote(("kback", g, i, n), src, dst, device(slab, core, to))

    def sum_stage1(g):
        g_buf[g, 0] = (gk[...] * SCALE).astype(BF)
        g_buf[g, 1] = gv[...].astype(BF)
        for i in range(4):
            core_sum(g, i).start()

    def sum_stage2(g):
        for i in range(2):
            core_sum(g, i).wait_recv()
            at = pl.multiple_of((core + 2 * i) * UNIT, UNIT)
            z_send[g, i] = (g_buf[g, :, pl.ds(at, UNIT), :].astype(F32) + core_buf[g, i].astype(F32)).astype(BF)
        for step in range(1, 4):
            z_sum(g, step).start()
        core_sum(g, 2).wait_recv()
        core_sum(g, 3).wait_recv()
        a = core_buf[g, 2].astype(F32)
        b = core_buf[g, 3].astype(F32)
        lower = core == 0
        far = g_buf[g, :, slot[0]:slot[0] + UNIT, :].astype(F32)
        near = g_buf[g, :, slot[2]:slot[2] + UNIT, :].astype(F32)
        here = g_buf[g, :, slot[4]:slot[4] + UNIT, :].astype(F32)
        w_send[g, 0] = (near + jnp.where(lower, a, b)).astype(BF)
        w_send[g, 1] = (far + jnp.where(lower, 0.0, a)).astype(BF)
        sum_buf[g] = here + jnp.where(lower, b, 0.0)
        for back in (1, 2):
            @pl.when(slab >= back)
            def _():
                w_sum(g, back).start()

    def sum_stage3(g):
        for step in range(1, 4):
            z_sum(g, step).wait_recv()
        at = pl.multiple_of((z % 2) * 4 * PART, 4 * PART)
        total = z_send[g, z // 2, :, pl.ds(at, 4 * PART), :].astype(F32)
        for i in range(3):
            total += z_buf[g, i].astype(F32)
        x_send[g] = total.astype(BF)
        for step in range(1, 4):
            x_sum(g, step).start()

    def sum_stage4(g):
        for step in range(1, 4):
            x_sum(g, step).wait_recv()
        total = x_send[g, :, pl.ds(pl.multiple_of(x * PART, PART), PART), :].astype(F32)
        for i in range(3):
            total += x_buf[g, i].astype(F32)
        last_send[g] = total.astype(BF)

        @pl.when(slab != origin)
        def _():
            home(g).start()

    def sum_stage5(g):
        for back in (1, 2):
            @pl.when(slab + back < 16)
            def _():
                w_sum(g, back).wait_recv()
                sum_buf[g] += w_buf[g, back - 1].astype(F32)

        @pl.when(source)
        def _():
            for i in range(8):
                @pl.when(8 * x + i != slab)
                def _():
                    arrival(g, i).wait_recv()

            @pl.when(slab == 0)
            def _():
                last_buf[g, :, 0:PART, :] = last_send[g]

            sum_buf[g] += last_buf[g].astype(F32)

        k_buf[g] = sum_buf[g].astype(BF)
        for i in range(4):
            for n in range(2):
                k_back(g, i, n).start()


    def hook(u, stage):
        g = u // 2
        if stage == 0:
            if u % 2 == 0:
                kv_stage6(g)
            for i in ((0, 1), (2, 3))[u % 2]:
                for n in range(2):
                    if i == 3:
                        q_head(g, i, n).wait()
                    else:
                        q_head(g, i, n).wait_recv()
        if stage == 2 or stage == 3:
            for i in ((0, 1), (2, 3))[u % 2]:
                q_back(g, i, stage - 2).start()
        if (u, stage) == (0, 1):
            kv_stage4(1)
            kv_stage5(1)
        if (u, stage) == (1, 3):
            sum_stage1(0)
        if (u, stage) == (2, 1):
            sum_stage2(0)
        if (u, stage) == (2, 3):
            sum_stage3(0)
        if (u, stage) == (3, 2):
            sum_stage4(0)
        if (u, stage) == (3, 3):
            sum_stage1(1)
            sum_stage5(0)
            sum_stage2(1)
            sum_stage3(1)
            sum_stage4(1)
            sum_stage5(1)

    def hooks(u, stage):
        for k in range(2 * GROUPS):
            @pl.when(u == k)
            def _():
                hook(k, stage)

    kv_start(0)
    kv_start(1)
    q_start(0)
    kv_stage1(0)
    kv_stage1(1)
    kv_stage2(0)
    kv_stage2(1)
    kv_stage3(0)
    kv_stage3(1)
    q_start(1)
    kv_stage4(0)
    kv_stage5(0)


    first = ctx * UNIT
    base = first - BACK * UNIT - PRE

    def unit(u, carry):
        g = u // 2
        late = y // 2
        r = jnp.where(u % 2 == 0, 1 - late, late)
        row_at = pl.multiple_of(r * ROWS, ROWS)
        w_at = pl.multiple_of(PRE + r * ROWS, ROWS)
        hooks(u, 0)

        @pl.when(u % 2 == 0)
        def _():
            for n in range(2):
                kt[n] = kv[g, n].astype(F32).T.astype(BF)
            gk[...] = jnp.zeros_like(gk)
            gv[...] = jnp.zeros_like(gv)

        pos = first + r * ROWS + lax.broadcasted_iota(jnp.int32, (1, LANES), 1) % ROWS
        start_i = jnp.zeros((1, LANES), jnp.int32)
        share_i = jnp.zeros((1, LANES), jnp.int32)
        begin = lens[0]
        for d in range(1, DOCS):
            inside = pos >= begin
            start_i = jnp.where(inside, begin, start_i)
            share_i = jnp.where(inside, share[d], share_i)
            begin = begin + lens[d]
        lim = jnp.where(share_i == 1, lens[0], 0)
        low = start_i - base - w_at
        high = pos - base - w_at

        blocks = []
        for at in range(0, PRE, KC):
            blocks.append((at, at, KC))
        for at in range(0, BACK * UNIT, KC):
            blocks.append((pl.multiple_of(w_at + at, ROWS), PRE + at, KC))
        blocks.append((pl.multiple_of(w_at + BACK * UNIT, ROWS), PRE + BACK * UNIT, ROWS))

        for h in range(PER):
            q_scr[h * ROWS:(h + 1) * ROWS, :] = q_in[g, pl.ds(row_at, ROWS), h * HD:(h + 1) * HD]
        top = jnp.full((8, LANES), -1e30, F32)
        for src, at, count in blocks:
            s = lax.dot_general(kv[g, 0, pl.ds(src, count), :], q_scr[...], NT, preferred_element_type=F32)
            j = lax.broadcasted_iota(jnp.int32, (count, LANES), 0)
            if at < PRE:
                ok = j < lim - at
            else:
                ok = j >= low - (at - PRE)
                if count == ROWS:
                    ok &= j <= high - (at - PRE)
            s = jnp.where(ok, s, -1e30)
            s_scr[at:at + count, :] = s
            top = jnp.maximum(top, jnp.max(s.reshape(count // 8, 8, LANES), axis=0))
        m_scr[...] = top
        hooks(u, 1)

        mc = jnp.max(m_scr[...], axis=0, keepdims=True) * (SCALE * LOG2E)
        total = jnp.zeros((8, LANES), F32)
        for src, at, count in blocks:
            p = jnp.exp2(s_scr[at:at + count, :] * (SCALE * LOG2E) - mc)
            total += jnp.sum(p.reshape(count // 8, 8, LANES), axis=0)
            pb = p.astype(BF)
            p_scr[at:at + count, :] = pb
            o = jnp.dot(kt[1, :, pl.ds(src, count)], pb, preferred_element_type=F32)
            if at == 0:
                acc[...] = o
            else:
                acc[...] += o
        inv = 1.0 / jnp.sum(total, axis=0, keepdims=True)
        out_t = acc[...] * inv
        out = out_t.T.astype(BF)
        parts = []
        for h in range(PER):
            out_buf[g, pl.ds(row_at, ROWS), h * HD:(h + 1) * HD] = out[h * ROWS:(h + 1) * ROWS, :]
            parts.append(do_in[g, pl.ds(row_at, ROWS), h * HD:(h + 1) * HD].astype(F32).T)
        do_t = (jnp.concatenate(parts, axis=1) * inv).astype(BF)
        dot_scr[...] = do_t
        l_scr[...] = jnp.sum(do_t.astype(F32) * out_t.astype(BF).astype(F32), axis=0, keepdims=True)
        hooks(u, 2)

        delta = l_scr[...]
        for src, at, count in blocks:
            dp = jnp.dot(kv[g, 1, pl.ds(src, count), :], dot_scr[...], preferred_element_type=F32)
            pb = p_scr[at:at + count, :]
            ds = (pb.astype(F32) * (dp - delta)).astype(BF)
            gv[pl.ds(src, count), :] += lax.dot_general(pb, dot_scr[...], NT, preferred_element_type=F32)
            gk[pl.ds(src, count), :] += jnp.dot(ds, q_scr[...], preferred_element_type=F32)
            o = jnp.dot(kt[0, :, pl.ds(src, count)], ds, preferred_element_type=F32)
            if at == 0:
                acc[...] = o
            else:
                acc[...] += o
        dq = (acc[...] * SCALE).T.astype(BF)
        for h in range(PER):
            dq_buf[g, pl.ds(row_at, ROWS), h * HD:(h + 1) * HD] = dq[h * ROWS:(h + 1) * ROWS, :]
        hooks(u, 3)
        return carry

    lax.fori_loop(0, 2 * GROUPS, unit, 0)


    for g in range(GROUPS):
        for n in range(2):
            for i in range(3):
                q_back(g, i, n).wait_recv()
                k_back(g, i, n).wait_recv()
            q_back(g, 3, n).wait()
            k_back(g, 3, n).wait()
        for n in range(2):
            for i in range(3):
                q_head(g, i, n).wait_send()
                kv_head(g, n * 4 + i).wait_send()
                q_back(g, i, n).wait_send()
                k_back(g, i, n).wait_send()
        for step in range(1, 4):
            along_x(g, step).wait_send()
            along_z(g, step).wait_send()
            z_sum(g, step).wait_send()
            x_sum(g, step).wait_send()
        for i in range(2):
            half(g, i).wait_send()
        for i in range(4):
            core_sum(g, i).wait_send()

        @pl.when(source)
        def _():
            for i in range(8):
                @pl.when(8 * x + i != slab)
                def _():
                    scatter(g, i).wait_send()

        for ahead in (1, 2):
            @pl.when(slab + ahead < 16)
            def _():
                window(g, ahead).wait_send()

            @pl.when(slab >= ahead)
            def _():
                w_sum(g, ahead).wait_send()

        @pl.when(core == 0)
        def _():
            core_own(g).wait_send()

            @pl.when(slab >= 1)
            def _():
                near_up(g).wait_send()

        @pl.when(core == 1)
        def _():
            @pl.when(slab >= 1)
            def _():
                near_down(g).wait_send()

            @pl.when(slab >= 2)
            def _():
                far_down(g).wait_send()

        @pl.when(slab != origin)
        def _():
            home(g).wait_send()

    assert sum(c for _, c in table.values()) <= SEMS


def on_device(queries, keys, values, grad_out, doc_lengths, share_prefix):
    anywhere = pl.BlockSpec(memory_space=pl.ANY)
    smem = pl.BlockSpec(memory_space=pltpu.SMEM)
    unit = (2, UNIT, HD)
    G = GROUPS
    return tuple(pl.pallas_call(
        kernel,
        in_specs=[smem, smem] + [anywhere] * 4,
        out_specs=[anywhere] * 4,
        out_shape=[
            jax.ShapeDtypeStruct((BLK, QH * HD), BF),
            jax.ShapeDtypeStruct((BLK, QH * HD), BF),
            jax.ShapeDtypeStruct((BLK, KVH * HD), BF),
            jax.ShapeDtypeStruct((BLK, KVH * HD), BF),
        ],
        scratch_shapes=[
            pltpu.VMEM((G, UNIT, WIDE), BF),
            pltpu.VMEM((G, UNIT, WIDE), BF),
            pltpu.VMEM((G, 2, KEYS, HD), BF),
            pltpu.VMEM((2, HD, KEYS), BF),
            pltpu.VMEM((SEEN, LANES), F32),
            pltpu.VMEM((SEEN, LANES), BF),
            pltpu.VMEM((LANES, HD), BF),
            pltpu.VMEM((HD, LANES), BF),
            pltpu.VMEM((HD, LANES), F32),
            pltpu.VMEM((8, LANES), F32),
            pltpu.VMEM((1, LANES), F32),
            pltpu.VMEM((KEYS, HD), F32),
            pltpu.VMEM((KEYS, HD), F32),
            pltpu.VMEM((G, UNIT, WIDE), BF),
            pltpu.VMEM((G, UNIT, WIDE), BF),
            pltpu.VMEM((G, 2, KEYS, HD), BF),
            pltpu.VMEM((G, 4) + unit, BF),
            pltpu.VMEM((G, 2) + unit, BF),
            pltpu.VMEM((G, 3, 2, 4 * PART, HD), BF),
            pltpu.VMEM((G, 2, 4 * PART, HD), BF),
            pltpu.VMEM((G, 3, 2, PART, HD), BF),
            pltpu.VMEM((G, 2, PART, HD), BF),
            pltpu.VMEM((G,) + unit, BF),
            pltpu.VMEM((G, 2) + unit, BF),
            pltpu.VMEM((G, 2) + unit, BF),
            pltpu.VMEM((G,) + unit, F32),
            pltpu.VMEM((G,) + unit, BF),
            pltpu.SemaphoreType.DMA((SEMS,)),
            pltpu.SemaphoreType.DMA((SEMS,)),
            pltpu.SemaphoreType.DMA((18,)),
        ],
        compiler_params=pltpu.CompilerParams(
            collective_id=0, has_side_effects=True, vmem_limit_bytes=60 * 1024 * 1024
        ),
        name="packed_attention",
    )(doc_lengths, share_prefix, queries, grad_out, keys, values))


def solution(mesh):
    rows = P(("ctx", "heads"), None)
    return jax.shard_map(
        on_device, mesh=mesh, in_specs=(rows, rows, rows, rows, P(), P()),
        out_specs=(rows, rows, rows, rows), check_vma=False,
    )
```

time: 619 us -> 100 us (0.16); the launches traced: 626 us -> 99.9 us
  waiting for transfers between devices: 298 us -> 0 us
  local copies, waits for them, and re-layouts: 168 us -> 4.98 us
  Pallas kernels: 0 us -> 94.3 us
  other arithmetic: 45.5 us -> 0 us
  matrix products: 35.4 us -> 0 us
  starting transfers between devices: 24.3 us -> 0 us
  loops' own time: 21.2 us -> 0 us
  blocking collectives: 19.4 us -> 0 us
  between operations: 13.9 us -> 0.65 us
    reduce_scatter x2 -> x0, waiting for transfers between devices: 221 us -> none  [the longest x1 130 us: on_device(): lax.psum_scatter(k_terms, 'ctx', scatter_dimension=0, tiled=True)]
    dynamic_update_slice x48 -> x0, local copies, waits for them, and re-layouts: 102 us -> none  [on_device(): lax.scan(back_step, jnp.zeros((tok, groups, per, HD), jnp.float32), (k_st...]
    pallas_call x0 -> x1, Pallas kernels: none -> 94.3 us  [on_device(): pl.pallas_call(kernel, in_specs=[smem, smem] + [anywhere] * 4, out_specs=...]
    all_gather x2 -> x0, waiting for transfers between devices: 40.4 us -> none  [the longest x1 40.4 us: on_device(): lax.all_gather(v_loc, 'ctx', axis=0, tiled=True)]
    all_to_all x6 -> x0, waiting for transfers between devices: 36.8 us -> none  [the longest x1 13.4 us: on_device(): lax.all_to_all(out_rows, 'heads', split_axis=0, concat_axis=1, tiled=True)]
    dot_general x14 -> x0, matrix products: 35.4 us -> none  [the longest x2 6.96 us: back_compute(): jnp.einsum('gjts,tgjd->sgd', prob.astype(jnp.bfloat16), do_four, preferre...]
    reduce_or x32 -> x0, other arithmetic: 30.1 us -> none  [the longest x16 15.5 us: back_step(): return lax.cond(jnp.any(allowed), back_compute, passby, grad_q)]
    broadcast_in_dim x30 -> x0, local copies, waits for them, and re-layouts: 24.6 us -> none  [the longest x28 24.6 us: on_device(): lax.scan(back_step, jnp.zeros((tok, groups, per, HD), jnp.float32), (k_st...]
  transfers between devices with their start and end apart: 10 -> 0, of which waited for: 7 -> 0; matrix products, arithmetic and copies ran while one was open for 4% -> 0% of each run, Pallas kernels for 0% -> 0%
where the time goes in v2:
time: 100 us; the launch traced here: 99.9 us
  Pallas kernels  94.3 us (94%)
  local copies, waits for them, and re-layouts  4.98 us (5%)
    pallas_call x1, Pallas kernels, on_device(): pl.pallas_call(kernel, in_specs=[smem, smem] + [anywhere] * 4, out_specs=...  94.3 us
    unnamed x10, local copies, waits for them, and re-layouts  4.98 us

profile of v2, /device:TPU:2, one launch (start us, length us, event | category | flops | bytes accessed | tf_op | source)
XLA Modules:
  0.0 99.9 jit_solution(15106231316670653733)
XLA Ops:
  0.6 94.3 %packed_attention.1 = (bf16[64,8192]{1,0:T(8,128)(2,1)}, bf16[64,8192]{1,0:T(8,128)(2,1)}, bf16[64,1024]{1,0:T(8,128)(2,1)}, bf16[64,1024]{1,0:T(8,128)(2,1)}) custom-call(s32[16]{0:T(128)} %lens.1, s32[16]{0:T(128)} %share.1, bf16[64,8192]{1,0:T(8,128)(2,1)} %q_ref.1, bf16[64,8192]{1,0:T(8,128)(2,1)} %do_ref.1, bf16[64,1024]{1,0:T(8,128)(2,1)} %k_ref.1, ...), custom_call_target="tpu_custom_call" | custom-call | tf_op jit(solution)/shard_map/packed_attention/pallas_call | solution.py:641
  94.9 0.0 copy-start
  94.9 2.4 %copy.14 = bf16[64,8192]{1,0:T(8,128)(2,1)} copy(bf16[64,8192]{1,0:T(8,128)(2,1)} %get-tuple-element.8) | data formatting | bytes 2097152
  97.3 0.0 copy-done
  97.3 0.0 copy-start.2
  97.3 1.0 copy.15
  98.2 0.1 copy-done.2
  98.3 0.0 copy-start.1
  98.3 0.7 copy.16
  98.9 0.3 copy-done.1
  99.2 0.7 copy.17
Async XLA Ops:
  94.9 2.4 %copy-start = (bf16[64,8192]{1,0:T(8,128)(2,1)S(1)}, bf16[64,8192]{1,0:T(8,128)(2,1)}, u32[]{:S(2)}) copy-start(bf16[64,8192]{1,0:T(8,128)(2,1)} %get-tuple-element.9) | copy-start | bytes 3145732
  97.3 1.0 %copy-start.2 = (bf16[64,1024]{1,0:T(8,128)(2,1)S(1)}, bf16[64,1024]{1,0:T(8,128)(2,1)}, u32[]{:S(2)}) copy-start(bf16[64,1024]{1,0:T(8,128)(2,1)} %get-tuple-element.10) | copy-start | bytes 393220
  98.3 1.0 copy-start.1

commit v3 on v2

v3 whole, which is shorter than its diff:
```python
import jax
import jax.numpy as jnp
from jax import lax
from jax.experimental import pallas as pl
from jax.experimental.pallas import tpu as pltpu
from jax.sharding import PartitionSpec as P

QH = 64
KVH = 8
HD = 128
PER = QH // KVH
DOCS = 16
MESH = pl.DeviceIdType.MESH
BF = jnp.bfloat16
F32 = jnp.float32

UNIT = 256
BLK = 64
BACK = 4
PRE = 1024
KEYS = PRE + (BACK + 1) * UNIT
GROUPS = 2
WIDE = PER * HD

ROWS = 128
LANES = PER * ROWS
KC = 512
SPAN = BACK * UNIT + ROWS
SCALE = HD ** (-0.5)
LOG2E = 1.4426950408889634
QUARTER = UNIT // 4
SEMS = 160
NT = (((1,), (1,)), ((), ()))


def kernel(
    lens, share, q_ref, do_ref, k_ref, v_ref, o_ref, odq_ref, dk_ref, dv_ref,
    q_in, do_in, kv, kt, s_scr, p_win, p_pre, q_scr, dot_scr, acc, out_t, do_t, dq_t, lim, stat, gk, gv,
    out_buf, dq_buf, g_buf, core_buf, z_send, z_buf, x_send, x_buf, last_send, last_buf, w_send, w_buf,
    sum_buf, k_buf, send, recv, local,
):
    ctx = lax.axis_index("ctx")
    y = lax.axis_index("heads")
    core = ctx % 2
    slab = ctx // 2
    z = slab // 4
    x = slab % 4
    mine = pl.multiple_of(y * BLK, BLK)
    own = PRE + BACK * UNIT
    slot = [PRE + i * UNIT for i in range(BACK + 1)]
    first = ctx * UNIT
    base = first - BACK * UNIT - PRE

    def device(to_slab, to_core, to_y):
        return {"ctx": to_slab * 2 + to_core, "heads": to_y}

    sibling = device(slab, 1 - core, y)
    peers = [y + 1 - 2 * (y % 2), 3 - y, (y + 2) % 4]
    halves = [y // 2, 1 - y // 2]
    of_half = ((0, 3), (1, 2))

    @pl.when(slab < 2)
    def _():
        for g in range(GROUPS):
            kv[g, :, PRE:own, :] = jnp.zeros((2, BACK * UNIT, HD), BF)

    barrier = pltpu.get_barrier_semaphore()

    def greet(to):
        pl.semaphore_signal(barrier, inc=1, device_id=to, device_id_type=MESH)

    for step in range(1, 4):
        greet(device(z * 4 + (x + step) % 4, core, y))
        greet(device((slab + 4 * step) % 16, core, y))
        greet(device(slab, core, (y + step) % 4))
    for step in (1, 2, 14, 15):
        greet(device((slab + step) % 16, core, y))
    greet(sibling)

    for h in range(2):
        pos = first + halves[h] * ROWS + lax.broadcasted_iota(jnp.int32, (1, LANES), 1) % ROWS
        start_i = jnp.zeros((1, LANES), jnp.int32)
        share_i = jnp.zeros((1, LANES), jnp.int32)
        begin = lens[0]
        for d in range(1, DOCS):
            inside = pos >= begin
            start_i = jnp.where(inside, begin, start_i)
            share_i = jnp.where(inside, share[d], share_i)
            begin = begin + lens[d]
        w_at = PRE + halves[h] * ROWS
        lim[h, 0:1, :] = jnp.where(share_i == 1, lens[0], 0)
        lim[h, 1:2, :] = start_i - base - w_at
        lim[h, 2:3, :] = pos - base - w_at

    pl.semaphore_wait(barrier, 14)

    table = {}

    def number(name):
        return table.setdefault(name, len(table))

    def remote(name, src, dst, to, sent=None):
        at = number(name)
        out = at if sent is None else number(sent)
        return pltpu.make_async_remote_copy(
            src_ref=src, dst_ref=dst, send_sem=send.at[out], recv_sem=recv.at[at],
            device_id=to, device_id_type=MESH,
        )


    def kv_head(g, i, n):
        ref = (k_ref, v_ref)[n]
        to = (peers + [y])[i]
        src = ref.at[:, pl.ds(pl.multiple_of((to * GROUPS + g) * HD, HD), HD)]
        dst = kv.at[g, n, pl.ds(own + mine, BLK), :]
        if i == 3:
            return pltpu.make_async_copy(src, dst, local.at[g * 2 + n])
        return remote(("kv", g, i, n), src, dst, device(slab, core, to))

    def q_head(g, i, n):
        ref, into = ((q_ref, q_in), (do_ref, do_in))[n]
        to = (peers + [y])[i]
        src = ref.at[:, pl.ds(pl.multiple_of((to * GROUPS + g) * WIDE, WIDE), WIDE)]
        dst = into.at[g, pl.ds(mine, BLK), :]
        if i == 3:
            return pltpu.make_async_copy(src, dst, local.at[4 + g * 2 + n])
        return remote(("q", g, i, n), src, dst, device(slab, core, to))

    def rows(g, at, count):
        return kv.at[g, :, pl.ds(at, count), :]

    def move(name, g, src, dst, count, to):
        return remote((name, g), rows(g, src, count), rows(g, dst, count), to)

    def unit_at(u):
        return pl.multiple_of((core + 2 * u) * UNIT, UNIT)

    def z_quarter(g, step):
        to = (z + step) % 4
        return remote(
            ("quarter", g, step), rows(g, pl.multiple_of(own + to * QUARTER, QUARTER), QUARTER),
            rows(g, pl.multiple_of(unit_at(x) + to * QUARTER, QUARTER), QUARTER),
            device((slab + 4 * step) % 16, core, y),
        )

    def own_quarter(g):
        return pltpu.make_async_copy(
            rows(g, own, QUARTER), rows(g, pl.multiple_of(unit_at(x), QUARTER), QUARTER), local.at[8 + g]
        )

    def quarter_at(u):
        return pl.multiple_of(unit_at(u) + z * QUARTER, QUARTER)

    def x_quarter(g, u, step):
        at = quarter_at(u)
        return remote(
            ("x", g, u, step), rows(g, at, QUARTER), rows(g, at, QUARTER), device(z * 4 + (u + step) % 4, core, y),
            sent=("xs", g, step),
        )

    def z_all(g, u, step):
        at = quarter_at(u)
        return move(("z", u, step), g, at, at, QUARTER, device((slab + 4 * step) % 16, core, y))

    def half_unit(g, u):
        return move(("half", u), g, unit_at(u), unit_at(u), UNIT, sibling)

    def window(g, ahead):
        return move(
            ("window", ahead), g, own, slot[2] if ahead == 1 else slot[0], UNIT,
            device((slab + ahead) % 16, core, y),
        )

    def core_own(g):
        return move(("core", 3), g, own, slot[3], UNIT, sibling)

    def near_up(g):
        return move(("core", 1), g, slot[2], slot[1], UNIT, sibling)

    def near_down(g):
        return move(("core", 3), g, slot[2], slot[3], UNIT, sibling)

    def far_down(g):
        return move(("core", 1), g, slot[0], slot[1], UNIT, sibling)

    def q_start(g, n):
        for i in (0, 3, 1, 2):
            q_head(g, i, n).start()

    def q_wait(g, n):
        for i in range(4):
            if i == 3:
                q_head(g, i, n).wait()
            else:
                q_head(g, i, n).wait_recv()

    def kv_start(g):
        for i in range(4):
            for n in range(2):
                kv_head(g, i, n).start()

    def kv_units(g):
        for n in range(2):
            for i in range(3):
                kv_head(g, i, n).wait_recv()
            kv_head(g, 3, n).wait()
        for ahead in (1, 2):
            @pl.when(slab + ahead < 16)
            def _():
                window(g, ahead).start()

        @pl.when(slab < 2)
        def _():
            for step in range(1, 4):
                z_quarter(g, step).start()
            own_quarter(g).start()

        @pl.when(core == 0)
        def _():
            core_own(g).start()

    def pre_x(g):
        @pl.when(slab < 2)
        def _():
            own_quarter(g).wait()

        for step in range(1, 4):
            @pl.when((x < 2) & (z == step))
            def _():
                z_quarter(g, step).wait_recv()

        for u in range(2):
            @pl.when(x == u)
            def _():
                for step in range(1, 4):
                    x_quarter(g, u, step).start()

    def pre_z(g):
        for u in range(2):
            for step in range(1, 4):
                @pl.when(x == (u + step) % 4)
                def _():
                    x_quarter(g, u, step).wait_recv()
        for u in range(2):
            for step in range(1, 4):
                z_all(g, u, step).start()

    def pre_core(g):
        for u in range(2):
            for step in range(1, 4):
                z_all(g, u, step).wait_recv()
            half_unit(g, u).start()

    def pre_done(g):
        for u in range(2):
            half_unit(g, u).wait_recv()

    def win_core(g):
        @pl.when(slab >= 1)
        def _():
            window(g, 1).wait_recv()

            @pl.when(core == 0)
            def _():
                near_up(g).start()

            @pl.when(core == 1)
            def _():
                near_down(g).start()

        @pl.when(slab >= 2)
        def _():
            window(g, 2).wait_recv()

            @pl.when(core == 1)
            def _():
                far_down(g).start()

    def win_done(g):
        @pl.when(core == 1)
        def _():
            core_own(g).wait_recv()

            @pl.when(slab >= 1)
            def _():
                near_up(g).wait_recv()

        @pl.when(core == 0)
        def _():
            @pl.when(slab >= 1)
            def _():
                near_down(g).wait_recv()

            @pl.when(slab >= 2)
            def _():
                far_down(g).wait_recv()


    def q_back(g, i, n):
        buf, ref = ((out_buf, o_ref), (dq_buf, odq_ref))[n]
        to = (peers + [y])[i]
        src = buf.at[g, pl.ds(pl.multiple_of(to * BLK, BLK), BLK), :]
        dst = ref.at[:, pl.ds(pl.multiple_of((y * GROUPS + g) * WIDE, WIDE), WIDE)]
        if i == 3:
            return pltpu.make_async_copy(src, dst, local.at[10 + g * 2 + n])
        return remote(("back", g, i, n), src, dst, device(slab, core, to))

    def core_sum(g, i):
        at = unit_at(i) + (1 - 2 * core) * UNIT if i < 2 else slot[1 + 2 * (i - 2)]
        if i < 2:
            at = pl.multiple_of(at, UNIT)
        return remote(("csum", g, i), g_buf.at[g, :, pl.ds(at, UNIT), :], core_buf.at[g, i], sibling)

    def z_sum(g, step):
        at = pl.multiple_of(((z + step) % 4) * QUARTER, QUARTER)
        return remote(
            ("zsum", g, step), z_send.at[g, :, :, pl.ds(at, QUARTER), :], z_buf.at[g, step - 1],
            device((slab + 4 * step) % 16, core, y),
        )

    def x_sum(g, u, step):
        return remote(
            ("xsum", g, u, step), x_send.at[g, u], x_buf.at[g, step - 1], device(z * 4 + u, core, y),
        )

    def home(g, step):
        at = pl.multiple_of(z * QUARTER, QUARTER)
        return remote(
            ("home", g, step), last_send.at[g], last_buf.at[g, :, pl.ds(at, QUARTER), :], device(x, core, y),
        )

    def w_sum(g, back):
        return remote(
            ("wsum", g, back), w_send.at[g, back - 1], w_buf.at[g, back - 1],
            device((slab + 16 - back) % 16, core, y),
        )

    def k_back(g, i, n):
        ref = (dk_ref, dv_ref)[n]
        to = (peers + [y])[i]
        src = k_buf.at[g, n, pl.ds(pl.multiple_of(to * BLK, BLK), BLK), :]
        dst = ref.at[:, pl.ds(pl.multiple_of((y * GROUPS + g) * HD, HD), HD)]
        if i == 3:
            return pltpu.make_async_copy(src, dst, local.at[14 + g * 2 + n])
        return remote(("kback", g, i, n), src, dst, device(slab, core, to))

    def pre_sum_core(g):
        for i in range(2):
            core_sum(g, i).start()

    def pre_sum_z(g):
        for i in range(2):
            core_sum(g, i).wait_recv()
            z_send[g, i] = (
                g_buf[g, :, pl.ds(unit_at(i), UNIT), :].astype(F32) + core_buf[g, i].astype(F32)
            ).astype(BF)
        for step in range(1, 4):
            z_sum(g, step).start()

    def pre_sum_x(g):
        for step in range(1, 4):
            z_sum(g, step).wait_recv()
        total = z_send[g, :, :, pl.ds(pl.multiple_of(z * QUARTER, QUARTER), QUARTER), :].astype(F32)
        for i in range(3):
            total += z_buf[g, i].astype(F32)
        x_send[g] = total.astype(BF)
        for u in range(2):
            for step in range(1, 4):
                @pl.when(x == (u + step) % 4)
                def _():
                    x_sum(g, u, step).start()

    def pre_sum_home(g):
        for u in range(2):
            @pl.when(x == u)
            def _():
                total = x_send[g, u].astype(F32)
                for step in range(1, 4):
                    x_sum(g, u, step).wait_recv()
                    total += x_buf[g, step - 1].astype(F32)
                last_send[g] = total.astype(BF)
                for step in range(1, 4):
                    @pl.when(z == step)
                    def _():
                        home(g, step).start()

    def win_sum_core(g):
        for i in (2, 3):
            core_sum(g, i).start()

    def win_sum_x(g):
        core_sum(g, 2).wait_recv()
        core_sum(g, 3).wait_recv()
        a = core_buf[g, 2].astype(F32)
        b = core_buf[g, 3].astype(F32)
        lower = core == 0
        far = g_buf[g, :, slot[0]:slot[0] + UNIT, :].astype(F32)
        near = g_buf[g, :, slot[2]:slot[2] + UNIT, :].astype(F32)
        here = g_buf[g, :, slot[4]:slot[4] + UNIT, :].astype(F32)
        w_send[g, 1] = (far + jnp.where(lower, 0.0, a)).astype(BF)
        w_send[g, 0] = (near + jnp.where(lower, a, b)).astype(BF)
        for back in (2, 1):
            @pl.when(slab >= back)
            def _():
                w_sum(g, back).start()
        sum_buf[g] = here + jnp.where(lower, b, 0.0)

    def sum_back(g):
        @pl.when(slab < 2)
        def _():
            for step in range(1, 4):
                home_at = step * QUARTER
                remote(
                    ("home", g, step), last_send.at[g], last_buf.at[g, :, pl.ds(home_at, QUARTER), :], sibling
                ).wait_recv()
            last_buf[g, :, 0:QUARTER, :] = last_send[g]
            sum_buf[g] += last_buf[g].astype(F32)

        for back in (1, 2):
            @pl.when(slab + back < 16)
            def _():
                w_sum(g, back).wait_recv()
                sum_buf[g] += w_buf[g, back - 1].astype(F32)

        k_buf[g] = sum_buf[g].astype(BF)
        for i in (2, 1, 0, 3):
            for n in range(2):
                k_back(g, i, n).start()


    def blocks_of(part, h):
        if part == 0:
            return [(at, at, KC) for at in range(0, PRE, KC)]
        w_at = PRE + halves[h] * ROWS
        blocks = [(pl.multiple_of(w_at + at, ROWS), at, KC) for at in range(0, BACK * UNIT, KC)]
        return blocks + [(pl.multiple_of(w_at + BACK * UNIT, ROWS), BACK * UNIT, ROWS)]

    def place(h):
        return pl.ds(pl.multiple_of(halves[h] * ROWS, ROWS), ROWS)

    def scores(g, h, part, state):
        state["top"] = jnp.full((8, LANES), -1e30, F32)

        def step(src, at, count):
            s = lax.dot_general(
                kv[g, 0, pl.ds(src, count), :], q_scr[g, h], NT, preferred_element_type=F32
            )
            j = lax.broadcasted_iota(jnp.int32, (count, LANES), 0)
            if part == 0:
                ok = j < lim[h, 0:1, :] - at
            else:
                ok = j >= lim[h, 1:2, :] - at
                if count == ROWS:
                    ok &= j <= lim[h, 2:3, :] - at
            s = jnp.where(ok, s, -1e30)
            s_scr[h, at:at + count, :] = s
            state["top"] = jnp.maximum(state["top"], jnp.max(s.reshape(count // 8, 8, LANES), axis=0))

        return [lambda b=b: step(*b) for b in blocks_of(part, h)]

    def weighted(g, h, part, state):
        p_scr = (p_pre, p_win)[part]

        def step(src, at, count):
            if at == 0:
                state["mc"] = jnp.max(state["top"], axis=0, keepdims=True) * (SCALE * LOG2E)
                state["sum"] = jnp.zeros((8, LANES), F32)
            p = jnp.exp2(s_scr[h, at:at + count, :] * (SCALE * LOG2E) - state["mc"])
            state["sum"] += jnp.sum(p.reshape(count // 8, 8, LANES), axis=0)
            pb = p.astype(BF)
            p_scr[g, h, at:at + count, :] = pb
            o = jnp.dot(kt[g, 1, :, pl.ds(src, count)], pb, preferred_element_type=F32)
            spot = acc.at[part, g, h]
            if at == 0:
                spot[...] = o
            else:
                spot[...] += o

        return [lambda b=b: step(*b) for b in blocks_of(part, h)]

    def turn(g, low, count):
        for n in range(2):
            kt[g, n, :, low:low + count] = kv[g, n, low:low + count, :].astype(F32).T.astype(BF)

    def both(g, part):
        state = [{}, {}]
        for step in scores(g, 0, part, state[0]):
            step()
        late = scores(g, 1, part, state[1])
        for step in weighted(g, 0, part, state[0]):
            late.pop(0)()
            step()
        for step in weighted(g, 1, part, state[1]):
            step()
        return state

    def window_forward(g):
        for h in range(2):
            for i in range(PER):
                q_scr[g, h, i * ROWS:(i + 1) * ROWS, :] = q_in[g, place(h), i * HD:(i + 1) * HD]
        turn(g, PRE, KEYS - PRE)
        state = both(g, 1)
        for h in range(2):
            stat[g, h, 0:1, :] = state[h]["mc"]
            stat[g, h, 1:2, :] = jnp.sum(state[h]["sum"], axis=0, keepdims=True)

    def prefix_forward(g):
        turn(g, 0, PRE)
        state = both(g, 0)
        for h in range(2):
            mw = stat[g, h, 0:1, :]
            lw = stat[g, h, 1:2, :]
            mp = state[h]["mc"]
            lp = jnp.sum(state[h]["sum"], axis=0, keepdims=True)
            m = jnp.maximum(mw, mp)
            aw = jnp.exp2(mw - m)
            ap = jnp.exp2(mp - m)
            inv = 1.0 / (aw * lw + ap * lp)
            fp = ap * inv
            fw = aw * inv
            stat[g, h, 0:1, :] = fp
            stat[g, h, 1:2, :] = fw
            o = acc[0, g, h] * fp + acc[1, g, h] * fw
            out_t[g, h] = o.astype(BF)
            out = o.T.astype(BF)
            for i in range(PER):
                out_buf[g, place(h), i * HD:(i + 1) * HD] = out[i * ROWS:(i + 1) * ROWS, :]

    def gradients(g, h, part):
        p_scr = (p_pre, p_win)[part]
        if part == 0:
            for i in range(PER):
                do_t[g, h, :, i * ROWS:(i + 1) * ROWS] = (
                    do_in[g, place(h), i * HD:(i + 1) * HD].astype(F32).T.astype(BF)
                )
        factor = stat[g, h, part:part + 1, :]
        scaled = (do_t[g, h].astype(F32) * factor).astype(BF)
        dot_scr[h] = scaled
        delta = jnp.sum(scaled.astype(F32) * out_t[g, h].astype(F32), axis=0, keepdims=True)
        first_half = h == (0 if part == 0 else 1)
        for src, at, count in blocks_of(part, h):
            dp = jnp.dot(kv[g, 1, pl.ds(src, count), :], dot_scr[h], preferred_element_type=F32)
            pb = p_scr[g, h, at:at + count, :]
            ds = (pb.astype(F32) * (dp - delta)).astype(BF)
            tv = lax.dot_general(pb, dot_scr[h], NT, preferred_element_type=F32)
            tk = jnp.dot(ds, q_scr[g, h], preferred_element_type=F32)
            if first_half:
                gv[pl.ds(src, count), :] = tv
                gk[pl.ds(src, count), :] = tk
            else:
                g_buf[g, 1, pl.ds(src, count), :] = (gv[pl.ds(src, count), :] + tv).astype(BF)
                g_buf[g, 0, pl.ds(src, count), :] = ((gk[pl.ds(src, count), :] + tk) * SCALE).astype(BF)
            o = jnp.dot(kt[g, 0, :, pl.ds(src, count)], ds, preferred_element_type=F32)
            spot = dq_t.at[g, h]
            if part == 0 and at == 0:
                spot[...] = o
            else:
                spot[...] += o

    def prefix_backward(g):
        for h in range(2):
            gradients(g, h, 0)

    def window_backward(g, h):
        apart = [pl.ds(pl.multiple_of(PRE + halves[1 - i] * SPAN, ROWS), ROWS) for i in range(2)]
        if h == 1:
            zero = jnp.zeros((ROWS, HD), F32)
            gk[apart[1], :] = zero
            gv[apart[1], :] = zero
        gradients(g, h, 1)
        if h == 0:
            g_buf[g, 1, apart[0], :] = gv[apart[0], :].astype(BF)
            g_buf[g, 0, apart[0], :] = (gk[apart[0], :] * SCALE).astype(BF)
        dq = (dq_t[g, h] * SCALE).T.astype(BF)
        for i in range(PER):
            dq_buf[g, place(h), i * HD:(i + 1) * HD] = dq[i * ROWS:(i + 1) * ROWS, :]


    def each_group(before, work, after):
        def body(g, carry):
            for k in range(GROUPS):
                @pl.when(g == k)
                def _():
                    before(k)
            work(g)
            for k in range(GROUPS):
                @pl.when(g == k)
                def _():
                    after(k)
            return carry

        lax.fori_loop(0, GROUPS, body, 0)

    kv_start(0)
    kv_start(1)
    q_start(0, 0)
    kv_units(0)
    kv_units(1)
    q_start(1, 0)
    pre_x(0)
    pre_x(1)
    q_start(0, 1)
    q_start(1, 1)
    pre_z(0)
    win_core(0)

    def before_wf(g):
        if g == 1:
            win_core(1)
        q_wait(g, 0)
        win_done(g)

    def after_wf(g):
        if g == 0:
            pre_z(1)
            pre_core(0)

    each_group(before_wf, window_forward, after_wf)

    def before_pf(g):
        if g == 0:
            pre_core(1)
        pre_done(g)

    def after_pf(g):
        for i in (1, 2, 0, 3):
            q_back(g, i, 0).start()

    each_group(before_pf, prefix_forward, after_pf)

    def before_pb(g):
        q_wait(g, 1)

    def after_pb(g):
        pre_sum_core(g)
        if g == 1:
            pre_sum_z(0)

    each_group(before_pb, prefix_backward, after_pb)

    def after_wb(g, h):
        for i in of_half[h]:
            q_back(g, i, 1).start()
        if (g, h) == (0, 1):
            pre_sum_z(1)
        if (g, h) == (0, 0):
            win_sum_core(0)
            pre_sum_x(0)
        if (g, h) == (1, 1):
            pre_sum_x(1)
            win_sum_x(0)
            pre_sum_home(0)
        if (g, h) == (1, 0):
            win_sum_core(1)
            pre_sum_home(1)
            win_sum_x(1)
            sum_back(0)
            sum_back(1)

    def wb_body(g, carry):
        for h in (1, 0):
            window_backward(g, h)
            for k in range(GROUPS):
                @pl.when(g == k)
                def _():
                    after_wb(k, h)
        return carry

    lax.fori_loop(0, GROUPS, wb_body, 0)


    for g in range(GROUPS):
        for n in range(2):
            for i in range(3):
                q_back(g, i, n).wait_recv()
                k_back(g, i, n).wait_recv()
            q_back(g, 3, n).wait()
            k_back(g, 3, n).wait()
        for n in range(2):
            for i in range(3):
                q_head(g, i, n).wait_send()
                kv_head(g, i, n).wait_send()
                q_back(g, i, n).wait_send()
                k_back(g, i, n).wait_send()
        for step in range(1, 4):
            z_sum(g, step).wait_send()
            for u in range(2):
                z_all(g, u, step).wait_send()

                @pl.when(x == u)
                def _():
                    x_quarter(g, u, step).wait_send()

                @pl.when(x == (u + step) % 4)
                def _():
                    x_sum(g, u, step).wait_send()

            @pl.when((x < 2) & (z == step))
            def _():
                home(g, step).wait_send()

            @pl.when(slab < 2)
            def _():
                z_quarter(g, step).wait_send()
        for u in range(2):
            half_unit(g, u).wait_send()
        for i in range(4):
            core_sum(g, i).wait_send()

        for ahead in (1, 2):
            @pl.when(slab + ahead < 16)
            def _():
                window(g, ahead).wait_send()

            @pl.when(slab >= ahead)
            def _():
                w_sum(g, ahead).wait_send()

        @pl.when(core == 0)
        def _():
            core_own(g).wait_send()

            @pl.when(slab >= 1)
            def _():
                near_up(g).wait_send()

        @pl.when(core == 1)
        def _():
            @pl.when(slab >= 1)
            def _():
                near_down(g).wait_send()

            @pl.when(slab >= 2)
            def _():
                far_down(g).wait_send()

    assert len(table) <= SEMS, len(table)


def on_device(queries, keys, values, grad_out, doc_lengths, share_prefix):
    anywhere = pl.BlockSpec(memory_space=pl.ANY)
    smem = pl.BlockSpec(memory_space=pltpu.SMEM)
    unit = (2, UNIT, HD)
    G = GROUPS
    return tuple(pl.pallas_call(
        kernel,
        in_specs=[smem, smem] + [anywhere] * 4,
        out_specs=[anywhere] * 4,
        out_shape=[
            jax.ShapeDtypeStruct((BLK, QH * HD), BF),
            jax.ShapeDtypeStruct((BLK, QH * HD), BF),
            jax.ShapeDtypeStruct((BLK, KVH * HD), BF),
            jax.ShapeDtypeStruct((BLK, KVH * HD), BF),
        ],
        scratch_shapes=[
            pltpu.VMEM((G, UNIT, WIDE), BF),
            pltpu.VMEM((G, UNIT, WIDE), BF),
            pltpu.VMEM((G, 2, KEYS, HD), BF),
            pltpu.VMEM((G, 2, HD, KEYS), BF),
            pltpu.VMEM((2, SPAN, LANES), F32),
            pltpu.VMEM((G, 2, SPAN, LANES), BF),
            pltpu.VMEM((G, 2, PRE, LANES), BF),
            pltpu.VMEM((G, 2, LANES, HD), BF),
            pltpu.VMEM((2, HD, LANES), BF),
            pltpu.VMEM((2, G, 2, HD, LANES), F32),
            pltpu.VMEM((G, 2, HD, LANES), BF),
            pltpu.VMEM((G, 2, HD, LANES), BF),
            pltpu.VMEM((G, 2, HD, LANES), F32),
            pltpu.VMEM((2, 8, LANES), jnp.int32),
            pltpu.VMEM((G, 2, 8, LANES), F32),
            pltpu.VMEM((KEYS, HD), F32),
            pltpu.VMEM((KEYS, HD), F32),
            pltpu.VMEM((G, UNIT, WIDE), BF),
            pltpu.VMEM((G, UNIT, WIDE), BF),
            pltpu.VMEM((G, 2, KEYS, HD), BF),
            pltpu.VMEM((G, 4) + unit, BF),
            pltpu.VMEM((G, 2) + unit, BF),
            pltpu.VMEM((G, 3, 2, 2, QUARTER, HD), BF),
            pltpu.VMEM((G, 2, 2, QUARTER, HD), BF),
            pltpu.VMEM((G, 3, 2, QUARTER, HD), BF),
            pltpu.VMEM((G, 2, QUARTER, HD), BF),
            pltpu.VMEM((G,) + unit, BF),
            pltpu.VMEM((G, 2) + unit, BF),
            pltpu.VMEM((G, 2) + unit, BF),
            pltpu.VMEM((G,) + unit, F32),
            pltpu.VMEM((G,) + unit, BF),
            pltpu.SemaphoreType.DMA((SEMS,)),
            pltpu.SemaphoreType.DMA((SEMS,)),
            pltpu.SemaphoreType.DMA((18,)),
        ],
        compiler_params=pltpu.CompilerParams(
            collective_id=0, has_side_effects=True, vmem_limit_bytes=60 * 1024 * 1024
        ),
        name="packed_attention",
    )(doc_lengths, share_prefix, queries, grad_out, keys, values))


def solution(mesh):
    rows = P(("ctx", "heads"), None)
    return jax.shard_map(
        on_device, mesh=mesh, in_specs=(rows, rows, rows, rows, P(), P()),
        out_specs=(rows, rows, rows, rows), check_vma=False,
    )
```

time: 100 us -> 91.5 us (0.915)
  Pallas kernels: 94.3 us -> 85.7 us
    pallas_call x1, Pallas kernels: 94.3 us -> 85.7 us  [on_device(): pl.pallas_call(kernel, in_specs=[smem, smem] + [anywhere] * 4, out_specs=...]
where the time goes in v3:
time: 91.5 us; the launch traced here: 91.3 us
  Pallas kernels  85.7 us (94%)
  local copies, waits for them, and re-layouts  4.98 us (5%)
    pallas_call x1, Pallas kernels, on_device(): pl.pallas_call(kernel, in_specs=[smem, smem] + [anywhere] * 4, out_specs=...  85.7 us
    unnamed x10, local copies, waits for them, and re-layouts  4.98 us

profile of v3, /device:TPU:2, one launch (start us, length us, event | category | flops | bytes accessed | tf_op | source)
XLA Modules:
  0.0 91.3 jit_solution(9327114018996919552)
XLA Ops:
  0.6 85.7 %packed_attention.1 = (bf16[64,8192]{1,0:T(8,128)(2,1)}, bf16[64,8192]{1,0:T(8,128)(2,1)}, bf16[64,1024]{1,0:T(8,128)(2,1)}, bf16[64,1024]{1,0:T(8,128)(2,1)}) custom-call(s32[16]{0:T(128)} %lens.1, s32[16]{0:T(128)} %share.1, bf16[64,8192]{1,0:T(8,128)(2,1)} %q_ref.1, bf16[64,8192]{1,0:T(8,128)(2,1)} %do_ref.1, bf16[64,1024]{1,0:T(8,128)(2,1)} %k_ref.1, ...), custom_call_target="tpu_custom_call" | custom-call | tf_op jit(solution)/shard_map/packed_attention/pallas_call | solution.py:745
  86.3 0.0 copy-start
  86.4 2.4 %copy.14 = bf16[64,8192]{1,0:T(8,128)(2,1)} copy(bf16[64,8192]{1,0:T(8,128)(2,1)} %get-tuple-element.8) | data formatting | bytes 2097152
  88.7 0.0 copy-done
  88.7 0.0 copy-start.2
  88.7 1.0 %copy.15 = bf16[64,8192]{1,0:T(8,128)(2,1)} copy(bf16[64,8192]{1,0:T(8,128)(2,1)S(1)} %copy-done) | data formatting | bytes 2097152
  89.7 0.1 copy-done.2
  89.7 0.0 copy-start.1
  89.7 0.7 copy.16
  90.4 0.3 copy-done.1
  90.7 0.7 copy.17
Async XLA Ops:
  86.3 2.4 %copy-start = (bf16[64,8192]{1,0:T(8,128)(2,1)S(1)}, bf16[64,8192]{1,0:T(8,128)(2,1)}, u32[]{:S(2)}) copy-start(bf16[64,8192]{1,0:T(8,128)(2,1)} %get-tuple-element.9) | copy-start | bytes 3145732
  88.7 1.0 %copy-start.2 = (bf16[64,1024]{1,0:T(8,128)(2,1)S(1)}, bf16[64,1024]{1,0:T(8,128)(2,1)}, u32[]{:S(2)}) copy-start(bf16[64,1024]{1,0:T(8,128)(2,1)} %get-tuple-element.10) | copy-start | bytes 393220
  89.7 1.0 %copy-start.1 = (bf16[64,1024]{1,0:T(8,128)(2,1)S(1)}, bf16[64,1024]{1,0:T(8,128)(2,1)}, u32[]{:S(2)}) copy-start(bf16[64,1024]{1,0:T(8,128)(2,1)} %get-tuple-element.11) | copy-start | bytes 393220

commit v4 on v3

--- a/solution.py
+++ b/solution.py
@@ -29,13 +29,13 @@
 SCALE = HD ** (-0.5)
 LOG2E = 1.4426950408889634
 QUARTER = UNIT // 4
-SEMS = 160
+SENDS, ARRIVALS = 49, 59
 NT = (((1,), (1,)), ((), ()))
 
 
 def kernel(
     lens, share, q_ref, do_ref, k_ref, v_ref, o_ref, odq_ref, dk_ref, dv_ref,
-    q_in, do_in, kv, kt, s_scr, p_win, p_pre, q_scr, dot_scr, acc, out_t, do_t, dq_t, lim, stat, gk, gv,
+    q_in, do_in, kv, kt, s_scr, p_win, p_pre, q_scr, dot_scr, acc, out_t, do_t, lim, stat, gk, gv,
     out_buf, dq_buf, g_buf, core_buf, z_send, z_buf, x_send, x_buf, last_send, last_buf, w_send, w_buf,
     sum_buf, k_buf, send, recv, local,
 ):
@@ -76,6 +76,20 @@
     for step in (1, 2, 14, 15):
         greet(device((slab + step) % 16, core, y))
     greet(sibling)
+    source = slab < 2
+    spreads = x < 2
+    alone = (z == 0) & (y == 0)
+
+    @pl.when(source)
+    def _():
+        for step in range(4):
+            @pl.when(jnp.logical_not(alone) | (step > 0))
+            def _():
+                greet(device(y * 4 + x, core, (y + step) % 4))
+
+    @pl.when(spreads & jnp.logical_not(alone))
+    def _():
+        greet(device(x, core, z))
 
     for h in range(2):
         pos = first + halves[h] * ROWS + lax.broadcasted_iota(jnp.int32, (1, LANES), 1) % ROWS
@@ -92,21 +106,31 @@
         lim[h, 1:2, :] = start_i - base - w_at
         lim[h, 2:3, :] = pos - base - w_at
 
-    pl.semaphore_wait(barrier, 14)
-
-    table = {}
-
-    def number(name):
-        return table.setdefault(name, len(table))
+    one = jnp.where(alone, 1, 0)
+    pl.semaphore_wait(barrier, 14 + jnp.where(source, 4 - one, 0) + jnp.where(spreads, 1 - one, 0))
+
+    sends, arrivals = {}, {}
 
     def remote(name, src, dst, to, sent=None):
-        at = number(name)
-        out = at if sent is None else number(sent)
+        at = arrivals.setdefault(name, len(arrivals))
+        out = sends.setdefault(name if sent is None else sent, len(sends))
         return pltpu.make_async_remote_copy(
             src_ref=src, dst_ref=dst, send_sem=send.at[out], recv_sem=recv.at[at],
             device_id=to, device_id_type=MESH,
         )
 
+    def arrived(name, size):
+        pltpu.make_async_copy(size, size, recv.at[arrivals[name]]).wait()
+
+    def left(name, size):
+        pltpu.make_async_copy(size, size, send.at[sends[name]]).wait()
+
+    def size_of(count):
+        return kv.at[0, 0, 0:count, :]
+
+
+    def columns(ref, to, g):
+        return ref.at[:, pl.ds(pl.multiple_of((to * GROUPS + g) * HD, HD), HD)]
 
     def kv_head(g, i, n):
         ref = (k_ref, v_ref)[n]
@@ -115,7 +139,7 @@
         dst = kv.at[g, n, pl.ds(own + mine, BLK), :]
         if i == 3:
             return pltpu.make_async_copy(src, dst, local.at[g * 2 + n])
-        return remote(("kv", g, i, n), src, dst, device(slab, core, to))
+        return remote(("kv", g), src, dst, device(slab, core, to))
 
     def q_head(g, i, n):
         ref, into = ((q_ref, q_in), (do_ref, do_in))[n]
@@ -124,7 +148,7 @@
         dst = into.at[g, pl.ds(mine, BLK), :]
         if i == 3:
             return pltpu.make_async_copy(src, dst, local.at[4 + g * 2 + n])
-        return remote(("q", g, i, n), src, dst, device(slab, core, to))
+        return remote(("q", g, n), src, dst, device(slab, core, to))
 
     def rows(g, at, count):
         return kv.at[g, :, pl.ds(at, count), :]
@@ -135,32 +159,30 @@
     def unit_at(u):
         return pl.multiple_of((core + 2 * u) * UNIT, UNIT)
 
-    def z_quarter(g, step):
-        to = (z + step) % 4
+    def spread_in(g, step, n):
+        src = columns((k_ref, v_ref)[n], (y + step) % 4, g)
+        dst = kv.at[g, n, pl.ds(pl.multiple_of(unit_at(x) + mine, BLK), BLK), :]
         return remote(
-            ("quarter", g, step), rows(g, pl.multiple_of(own + to * QUARTER, QUARTER), QUARTER),
-            rows(g, pl.multiple_of(unit_at(x) + to * QUARTER, QUARTER), QUARTER),
-            device((slab + 4 * step) % 16, core, y),
+            ("in",), src, dst, device(y * 4 + x, core, (y + step) % 4), sent=("ins", step > 0)
         )
 
-    def own_quarter(g):
+    def spread_own(g, n):
+        src = columns((k_ref, v_ref)[n], y, g)
         return pltpu.make_async_copy(
-            rows(g, own, QUARTER), rows(g, pl.multiple_of(unit_at(x), QUARTER), QUARTER), local.at[8 + g]
+            src, kv.at[g, n, pl.ds(pl.multiple_of(unit_at(x) + mine, BLK), BLK), :], local.at[18 + g * 2 + n]
         )
 
-    def quarter_at(u):
-        return pl.multiple_of(unit_at(u) + z * QUARTER, QUARTER)
-
-    def x_quarter(g, u, step):
-        at = quarter_at(u)
+    def quarter(u):
+        return kv.at[:, :, pl.ds(pl.multiple_of(unit_at(u) + z * QUARTER, QUARTER), QUARTER), :]
+
+    def along_x(u, step):
         return remote(
-            ("x", g, u, step), rows(g, at, QUARTER), rows(g, at, QUARTER), device(z * 4 + (u + step) % 4, core, y),
-            sent=("xs", g, step),
+            ("x", u, step), quarter(u), quarter(u), device(z * 4 + (u + step) % 4, core, y), sent=("xs",)
         )
 
-    def z_all(g, u, step):
-        at = quarter_at(u)
-        return move(("z", u, step), g, at, at, QUARTER, device((slab + 4 * step) % 16, core, y))
+    def along_z(g, u, step):
+        at = pl.multiple_of(unit_at(u) + z * QUARTER, QUARTER)
+        return move("z", g, at, at, QUARTER, device((slab + 4 * step) % 16, core, y))
 
     def half_unit(g, u):
         return move(("half", u), g, unit_at(u), unit_at(u), UNIT, sibling)
@@ -188,11 +210,8 @@
             q_head(g, i, n).start()
 
     def q_wait(g, n):
-        for i in range(4):
-            if i == 3:
-                q_head(g, i, n).wait()
-            else:
-                q_head(g, i, n).wait_recv()
+        arrived(("q", g, n), q_in.at[g, 0:3 * BLK, :])
+        q_head(g, 3, n).wait()
 
     def kv_start(g):
         for i in range(4):
@@ -200,55 +219,65 @@
                 kv_head(g, i, n).start()
 
     def kv_units(g):
+        arrived(("kv", g), size_of(6 * BLK))
         for n in range(2):
-            for i in range(3):
-                kv_head(g, i, n).wait_recv()
             kv_head(g, 3, n).wait()
         for ahead in (1, 2):
             @pl.when(slab + ahead < 16)
             def _():
                 window(g, ahead).start()
 
-        @pl.when(slab < 2)
-        def _():
-            for step in range(1, 4):
-                z_quarter(g, step).start()
-            own_quarter(g).start()
-
         @pl.when(core == 0)
         def _():
             core_own(g).start()
 
-    def pre_x(g):
-        @pl.when(slab < 2)
-        def _():
-            own_quarter(g).wait()
-
-        for step in range(1, 4):
-            @pl.when((x < 2) & (z == step))
-            def _():
-                z_quarter(g, step).wait_recv()
-
+    def pre_in():
+        @pl.when(source)
+        def _():
+            for g in range(GROUPS):
+                for n in range(2):
+                    @pl.when(jnp.logical_not(alone))
+                    def _():
+                        spread_in(g, 0, n).start()
+
+                    @pl.when(alone)
+                    def _():
+                        spread_own(g, n).start()
+
+                    for step in range(1, 4):
+                        spread_in(g, step, n).start()
+
+    def pre_x():
         for u in range(2):
             @pl.when(x == u)
             def _():
-                for step in range(1, 4):
-                    x_quarter(g, u, step).start()
-
-    def pre_z(g):
+                @pl.when(jnp.logical_not(alone))
+                def _():
+                    arrived(("in",), size_of(4 * BLK))
+
+                @pl.when(alone)
+                def _():
+                    for g in range(GROUPS):
+                        for n in range(2):
+                            spread_own(g, n).wait()
+
+                for step in (2, 1, 3):
+                    along_x(u, step).start()
+
+    def pre_z():
         for u in range(2):
             for step in range(1, 4):
                 @pl.when(x == (u + step) % 4)
                 def _():
-                    x_quarter(g, u, step).wait_recv()
+                    along_x(u, step).wait_recv()
+        for g in range(GROUPS):
+            for step in (2, 1, 3):
+                for u in range(2):
+                    along_z(g, u, step).start()
+
+    def pre_core(g):
+        arrived(("z", g), size_of(12 * QUARTER))
         for u in range(2):
-            for step in range(1, 4):
-                z_all(g, u, step).start()
-
-    def pre_core(g):
-        for u in range(2):
-            for step in range(1, 4):
-                z_all(g, u, step).wait_recv()
             half_unit(g, u).start()
 
     def pre_done(g):
@@ -303,7 +332,7 @@
         dst = ref.at[:, pl.ds(pl.multiple_of((y * GROUPS + g) * WIDE, WIDE), WIDE)]
         if i == 3:
             return pltpu.make_async_copy(src, dst, local.at[10 + g * 2 + n])
-        return remote(("back", g, i, n), src, dst, device(slab, core, to))
+        return remote(("back", g, n), src, dst, device(slab, core, to))
 
     def core_sum(g, i):
         at = unit_at(i) + (1 - 2 * core) * UNIT if i < 2 else slot[1 + 2 * (i - 2)]
@@ -314,19 +343,21 @@
     def z_sum(g, step):
         at = pl.multiple_of(((z + step) % 4) * QUARTER, QUARTER)
         return remote(
-            ("zsum", g, step), z_send.at[g, :, :, pl.ds(at, QUARTER), :], z_buf.at[g, step - 1],
+            ("zsum", g), z_send.at[g, :, :, pl.ds(at, QUARTER), :], z_buf.at[g, step - 1],
             device((slab + 4 * step) % 16, core, y),
         )
 
     def x_sum(g, u, step):
         return remote(
-            ("xsum", g, u, step), x_send.at[g, u], x_buf.at[g, step - 1], device(z * 4 + u, core, y),
+            ("xsum", g, step), x_send.at[g, u], x_buf.at[g, step - 1], device(z * 4 + u, core, y),
+            sent=("xsums", g, u),
         )
 
     def home(g, step):
         at = pl.multiple_of(z * QUARTER, QUARTER)
         return remote(
             ("home", g, step), last_send.at[g], last_buf.at[g, :, pl.ds(at, QUARTER), :], device(x, core, y),
+            sent=("homes", g),
         )
 
     def w_sum(g, back):
@@ -342,7 +373,7 @@
         dst = ref.at[:, pl.ds(pl.multiple_of((y * GROUPS + g) * HD, HD), HD)]
         if i == 3:
             return pltpu.make_async_copy(src, dst, local.at[14 + g * 2 + n])
-        return remote(("kback", g, i, n), src, dst, device(slab, core, to))
+        return remote(("kback", g), src, dst, device(slab, core, to))
 
     def pre_sum_core(g):
         for i in range(2):
@@ -358,8 +389,7 @@
             z_sum(g, step).start()
 
     def pre_sum_x(g):
-        for step in range(1, 4):
-            z_sum(g, step).wait_recv()
+        arrived(("zsum", g), z_buf.at[g])
         total = z_send[g, :, :, pl.ds(pl.multiple_of(z * QUARTER, QUARTER), QUARTER), :].astype(F32)
         for i in range(3):
             total += z_buf[g, i].astype(F32)
@@ -411,7 +441,8 @@
             for step in range(1, 4):
                 home_at = step * QUARTER
                 remote(
-                    ("home", g, step), last_send.at[g], last_buf.at[g, :, pl.ds(home_at, QUARTER), :], sibling
+                    ("home", g, step), last_send.at[g], last_buf.at[g, :, pl.ds(home_at, QUARTER), :], sibling,
+                    sent=("homes", g),
                 ).wait_recv()
             last_buf[g, :, 0:QUARTER, :] = last_send[g]
             sum_buf[g] += last_buf[g].astype(F32)
@@ -550,16 +581,7 @@
             else:
                 g_buf[g, 1, pl.ds(src, count), :] = (gv[pl.ds(src, count), :] + tv).astype(BF)
                 g_buf[g, 0, pl.ds(src, count), :] = ((gk[pl.ds(src, count), :] + tk) * SCALE).astype(BF)
-            o = jnp.dot(kt[g, 0, :, pl.ds(src, count)], ds, preferred_element_type=F32)
-            spot = dq_t.at[g, h]
-            if part == 0 and at == 0:
-                spot[...] = o
-            else:
-                spot[...] += o
-
-    def prefix_backward(g):
-        for h in range(2):
-            gradients(g, h, 0)
+            p_scr[g, h, at:at + count, :] = ds
 
     def window_backward(g, h):
         apart = [pl.ds(pl.multiple_of(PRE + halves[1 - i] * SPAN, ROWS), ROWS) for i in range(2)]
@@ -571,7 +593,12 @@
         if h == 0:
             g_buf[g, 1, apart[0], :] = gv[apart[0], :].astype(BF)
             g_buf[g, 0, apart[0], :] = (gk[apart[0], :] * SCALE).astype(BF)
-        dq = (dq_t[g, h] * SCALE).T.astype(BF)
+
+    def query_gradients(g, h):
+        w_at = pl.multiple_of(PRE + halves[h] * ROWS, ROWS)
+        o = jnp.dot(kt[g, 0, :, 0:PRE], p_pre[g, h], preferred_element_type=F32)
+        o += jnp.dot(kt[g, 0, :, pl.ds(w_at, SPAN)], p_win[g, h], preferred_element_type=F32)
+        dq = (o * SCALE).T.astype(BF)
         for i in range(PER):
             dq_buf[g, place(h), i * HD:(i + 1) * HD] = dq[i * ROWS:(i + 1) * ROWS, :]
 
@@ -591,17 +618,17 @@
 
         lax.fori_loop(0, GROUPS, body, 0)
 
+    pre_in()
     kv_start(0)
     kv_start(1)
     q_start(0, 0)
+    pre_x()
     kv_units(0)
     kv_units(1)
     q_start(1, 0)
-    pre_x(0)
-    pre_x(1)
+    pre_z()
     q_start(0, 1)
     q_start(1, 1)
-    pre_z(0)
     win_core(0)
 
     def before_wf(g):
@@ -612,7 +639,6 @@
 
     def after_wf(g):
         if g == 0:
-            pre_z(1)
             pre_core(0)
 
     each_group(before_wf, window_forward, after_wf)
@@ -628,69 +654,77 @@
 
     each_group(before_pf, prefix_forward, after_pf)
 
-    def before_pb(g):
-        q_wait(g, 1)
-
-    def after_pb(g):
-        pre_sum_core(g)
-        if g == 1:
+    def after_pb(g, h):
+        if h == 1:
+            pre_sum_core(g)
+        if (g, h) == (1, 0):
             pre_sum_z(0)
 
-    each_group(before_pb, prefix_backward, after_pb)
-
     def after_wb(g, h):
-        for i in of_half[h]:
-            q_back(g, i, 1).start()
         if (g, h) == (0, 1):
             pre_sum_z(1)
         if (g, h) == (0, 0):
             win_sum_core(0)
-            pre_sum_x(0)
         if (g, h) == (1, 1):
+            win_sum_x(0)
             pre_sum_x(1)
-            win_sum_x(0)
-            pre_sum_home(0)
         if (g, h) == (1, 0):
             win_sum_core(1)
+            pre_sum_home(0)
+
+    def after_dq(g, h):
+        if (g, h) == (1, 1):
+            win_sum_x(1)
+        for i in of_half[h]:
+            q_back(g, i, 1).start()
+        if (g, h) == (0, 1):
+            pre_sum_x(0)
+        if (g, h) == (1, 0):
             pre_sum_home(1)
-            win_sum_x(1)
             sum_back(0)
             sum_back(1)
 
+    def at_group(g, h, after):
+        for k in range(GROUPS):
+            @pl.when(g == k)
+            def _():
+                after(k, h)
+
+    def pb_body(g, carry):
+        for k in range(GROUPS):
+            @pl.when(g == k)
+            def _():
+                q_wait(k, 1)
+        for h in (0, 1):
+            gradients(g, h, 0)
+            at_group(g, h, after_pb)
+        return carry
+
     def wb_body(g, carry):
-        for h in (1, 0):
-            window_backward(g, h)
-            for k in range(GROUPS):
-                @pl.when(g == k)
-                def _():
-                    after_wb(k, h)
+        for work, after in ((window_backward, after_wb), (query_gradients, after_dq)):
+            for h in (1, 0):
+                work(g, h)
+                at_group(g, h, after)
         return carry
 
+    lax.fori_loop(0, GROUPS, pb_body, 0)
     lax.fori_loop(0, GROUPS, wb_body, 0)
 
 
     for g in range(GROUPS):
         for n in range(2):
-            for i in range(3):
-                q_back(g, i, n).wait_recv()
-                k_back(g, i, n).wait_recv()
+            arrived(("back", g, n), out_buf.at[g, 0:3 * BLK, :])
             q_back(g, 3, n).wait()
             k_back(g, 3, n).wait()
-        for n in range(2):
-            for i in range(3):
-                q_head(g, i, n).wait_send()
-                kv_head(g, i, n).wait_send()
-                q_back(g, i, n).wait_send()
-                k_back(g, i, n).wait_send()
+            left(("q", g, n), q_in.at[g, 0:3 * BLK, :])
+            left(("back", g, n), out_buf.at[g, 0:3 * BLK, :])
+        arrived(("kback", g), size_of(6 * BLK))
+        left(("kback", g), size_of(6 * BLK))
+        left(("kv", g), size_of(6 * BLK))
+        left(("z", g), size_of(12 * QUARTER))
+        left(("zsum", g), z_buf.at[g])
         for step in range(1, 4):
-            z_sum(g, step).wait_send()
             for u in range(2):
-                z_all(g, u, step).wait_send()
-
-                @pl.when(x == u)
-                def _():
-                    x_quarter(g, u, step).wait_send()
-
                 @pl.when(x == (u + step) % 4)
                 def _():
                     x_sum(g, u, step).wait_send()
@@ -699,9 +733,6 @@
             def _():
                 home(g, step).wait_send()
 
-            @pl.when(slab < 2)
-            def _():
-                z_quarter(g, step).wait_send()
         for u in range(2):
             half_unit(g, u).wait_send()
         for i in range(4):
@@ -734,7 +765,39 @@
             def _():
                 far_down(g).wait_send()
 
-    assert len(table) <= SEMS, len(table)
+    @pl.when(source)
+    def _():
+        left(("ins", True), size_of(12 * BLK))
+
+        @pl.when(jnp.logical_not(alone))
+        def _():
+            left(("ins", False), size_of(4 * BLK))
+
+    @pl.when(spreads)
+    def _():
+        left(("xs",), size_of(12 * QUARTER))
+
+    assert (len(sends), len(arrivals)) == (SENDS, ARRIVALS), (len(sends), len(arrivals))
+
+
+def store_kernel(*refs):
+    src, dst, held = refs[:4], refs[4:8], refs[8:12]
+    into, out = refs[12:]
+    parts = [(a, b * BLK // n, BLK // n, b) for a, n in enumerate((4, 4, 1, 1)) for b in range(n)]
+
+    def load(a, at, count, b):
+        return pltpu.make_async_copy(src[a].at[pl.ds(at, count)], held[a].at[pl.ds(at, count)], into.at[a, b])
+
+    def save(a, at, count, b):
+        return pltpu.make_async_copy(held[a].at[pl.ds(at, count)], dst[a].at[pl.ds(at, count)], out.at[a, b])
+
+    for part in parts:
+        load(*part).start()
+    for part in parts:
+        load(*part).wait()
+        save(*part).start()
+    for part in parts:
+        save(*part).wait()
 
 
 def on_device(queries, keys, values, grad_out, doc_lengths, share_prefix):
@@ -742,7 +805,7 @@
     smem = pl.BlockSpec(memory_space=pltpu.SMEM)
     unit = (2, UNIT, HD)
     G = GROUPS
-    return tuple(pl.pallas_call(
+    results = pl.pallas_call(
         kernel,
         in_specs=[smem, smem] + [anywhere] * 4,
         out_specs=[anywhere] * 4,
@@ -765,7 +828,6 @@
             pltpu.VMEM((2, G, 2, HD, LANES), F32),
             pltpu.VMEM((G, 2, HD, LANES), BF),
             pltpu.VMEM((G, 2, HD, LANES), BF),
-            pltpu.VMEM((G, 2, HD, LANES), F32),
             pltpu.VMEM((2, 8, LANES), jnp.int32),
             pltpu.VMEM((G, 2, 8, LANES), F32),
             pltpu.VMEM((KEYS, HD), F32),
@@ -784,15 +846,23 @@
             pltpu.VMEM((G, 2) + unit, BF),
             pltpu.VMEM((G,) + unit, F32),
             pltpu.VMEM((G,) + unit, BF),
-            pltpu.SemaphoreType.DMA((SEMS,)),
-            pltpu.SemaphoreType.DMA((SEMS,)),
-            pltpu.SemaphoreType.DMA((18,)),
+            pltpu.SemaphoreType.DMA((SENDS,)),
+            pltpu.SemaphoreType.DMA((ARRIVALS,)),
+            pltpu.SemaphoreType.DMA((22,)),
         ],
         compiler_params=pltpu.CompilerParams(
             collective_id=0, has_side_effects=True, vmem_limit_bytes=60 * 1024 * 1024
         ),
         name="packed_attention",
-    )(doc_lengths, share_prefix, queries, grad_out, keys, values))
+    )(doc_lengths, share_prefix, queries, grad_out, keys, values)
+    return tuple(pl.pallas_call(
+        store_kernel,
+        in_specs=[anywhere] * 4,
+        out_specs=[anywhere] * 4,
+        out_shape=[jax.ShapeDtypeStruct(a.shape, a.dtype) for a in results],
+        scratch_shapes=[pltpu.VMEM(a.shape, a.dtype) for a in results] + [pltpu.SemaphoreType.DMA((4, 4))] * 2,
+        name="store_results",
+    )(*results))
 
 
 def solution(mesh):

time: 91.5 us -> 88 us (0.962)
  local copies, waits for them, and re-layouts: 4.98 us -> 0 us
  Pallas kernels: 85.7 us -> 87 us
    unnamed x10 -> x0, local copies, waits for them, and re-layouts: 4.98 us -> none
    pallas_call x0 -> x1, Pallas kernels: none -> 2.62 us  [on_device(): pl.pallas_call(store_kernel, in_specs=[anywhere] * 4, out_specs=[anywhere...]
    pallas_call x1, Pallas kernels: 85.7 us -> 84.4 us  [on_device(): pl.pallas_call(kernel, in_specs=[smem, smem] + [anywhere] * 4, out_specs=...]
where the time goes in v4:
time: 88 us; the launch traced here: 87.8 us
  Pallas kernels  87 us (99%)
    pallas_call x1, Pallas kernels, on_device(): pl.pallas_call(kernel, in_specs=[smem, smem] + [anywhere] * 4, out_specs=...  84.4 us
    pallas_call x1, Pallas kernels, on_device(): pl.pallas_call(store_kernel, in_specs=[anywhere] * 4, out_specs=[anywhere...  2.62 us

profile of v4, /device:TPU:2, one launch (start us, length us, event | category | flops | bytes accessed | tf_op | source)
XLA Modules:
  0.0 87.8 jit_solution(5561245260194544467)
XLA Ops:
  0.6 84.4 %packed_attention.1 = (bf16[64,8192]{1,0:T(8,128)(2,1)}, bf16[64,8192]{1,0:T(8,128)(2,1)}, bf16[64,1024]{1,0:T(8,128)(2,1)}, bf16[64,1024]{1,0:T(8,128)(2,1)}) custom-call(s32[16]{0:T(128)} %lens.1, s32[16]{0:T(128)} %share.1, bf16[64,8192]{1,0:T(8,128)(2,1)} %q_ref.1, bf16[64,8192]{1,0:T(8,128)(2,1)} %do_ref.1, bf16[64,1024]{1,0:T(8,128)(2,1)} %k_ref.1, ...), custom_call_target="tpu_custom_call" | custom-call | tf_op jit(solution)/shard_map/packed_attention/pallas_call | solution.py:808
  85.0 2.6 %store_results.1 = (bf16[64,8192]{1,0:T(8,128)(2,1)}, bf16[64,8192]{1,0:T(8,128)(2,1)}, bf16[64,1024]{1,0:T(8,128)(2,1)}, bf16[64,1024]{1,0:T(8,128)(2,1)}) custom-call(bf16[64,8192]{1,0:T(8,128)(2,1)} %get-tuple-element.8.refs_0_, bf16[64,8192]{1,0:T(8,128)(2,1)} %get-tuple-element.9.refs_1_, bf16[64,1024]{1,0:T(8,128)(2,1)} %get-tuple-element.10.refs_2_, ...), custom_call_target="tpu_custom_call" | custom-call | tf_op jit(solution)/shard_map/store_results/pallas_call | solution.py:858

commit v5 on v4

--- a/solution.py
+++ b/solution.py
@@ -624,9 +624,9 @@
     q_start(0, 0)
     pre_x()
     kv_units(0)
-    kv_units(1)
     q_start(1, 0)
     pre_z()
+    kv_units(1)
     q_start(0, 1)
     q_start(1, 1)
     win_core(0)
@@ -666,7 +666,6 @@
         if (g, h) == (0, 0):
             win_sum_core(0)
         if (g, h) == (1, 1):
-            win_sum_x(0)
             pre_sum_x(1)
         if (g, h) == (1, 0):
             win_sum_core(1)
@@ -679,6 +678,8 @@
             q_back(g, i, 1).start()
         if (g, h) == (0, 1):
             pre_sum_x(0)
+        if (g, h) == (0, 0):
+            win_sum_x(0)
         if (g, h) == (1, 0):
             pre_sum_home(1)
             sum_back(0)

time: 88 us -> 84.5 us (0.960)
  Pallas kernels: 87 us -> 83.6 us
    pallas_call x1, Pallas kernels: 84.4 us -> 81 us  [on_device(): pl.pallas_call(kernel, in_specs=[smem, smem] + [anywhere] * 4, out_specs=...]
where the time goes in v5:
time: 84.5 us; the launch traced here: 84.4 us
  Pallas kernels  83.6 us (99%)
    pallas_call x1, Pallas kernels, on_device(): pl.pallas_call(kernel, in_specs=[smem, smem] + [anywhere] * 4, out_specs=...  81 us
    pallas_call x1, Pallas kernels, on_device(): pl.pallas_call(store_kernel, in_specs=[anywhere] * 4, out_specs=[anywhere...  2.62 us

profile of v5, /device:TPU:2, one launch (start us, length us, event | category | flops | bytes accessed | tf_op | source)
XLA Modules:
  0.0 84.4 jit_solution(11948493363599232206)
XLA Ops:
  0.6 81.0 %packed_attention.1 = (bf16[64,8192]{1,0:T(8,128)(2,1)}, bf16[64,8192]{1,0:T(8,128)(2,1)}, bf16[64,1024]{1,0:T(8,128)(2,1)}, bf16[64,1024]{1,0:T(8,128)(2,1)}) custom-call(s32[16]{0:T(128)} %lens.1, s32[16]{0:T(128)} %share.1, bf16[64,8192]{1,0:T(8,128)(2,1)} %q_ref.1, bf16[64,8192]{1,0:T(8,128)(2,1)} %do_ref.1, bf16[64,1024]{1,0:T(8,128)(2,1)} %k_ref.1, ...), custom_call_target="tpu_custom_call" | custom-call | tf_op jit(solution)/shard_map/packed_attention/pallas_call | solution.py:809
  81.6 2.6 %store_results.1 = (bf16[64,8192]{1,0:T(8,128)(2,1)}, bf16[64,8192]{1,0:T(8,128)(2,1)}, bf16[64,1024]{1,0:T(8,128)(2,1)}, bf16[64,1024]{1,0:T(8,128)(2,1)}) custom-call(bf16[64,8192]{1,0:T(8,128)(2,1)} %get-tuple-element.8.refs_0_, bf16[64,8192]{1,0:T(8,128)(2,1)} %get-tuple-element.9.refs_1_, bf16[64,1024]{1,0:T(8,128)(2,1)} %get-tuple-element.10.refs_2_, ...), custom_call_target="tpu_custom_call" | custom-call | tf_op jit(solution)/shard_map/store_results/pallas_call | solution.py:859

commit v6 on v5

--- a/solution.py
+++ b/solution.py
@@ -624,9 +624,9 @@
     q_start(0, 0)
     pre_x()
     kv_units(0)
-    q_start(1, 0)
     pre_z()
     kv_units(1)
+    q_start(1, 0)
     q_start(0, 1)
     q_start(1, 1)
     win_core(0)
@@ -680,8 +680,9 @@
             pre_sum_x(0)
         if (g, h) == (0, 0):
             win_sum_x(0)
+        if (g, h) == (1, 1):
+            pre_sum_home(1)
         if (g, h) == (1, 0):
-            pre_sum_home(1)
             sum_back(0)
             sum_back(1)
 

time: 84.5 us -> 84.5 us (level)
  no operation moved by 1% of the time
where the time goes in v6:
time: 84.5 us; the launch traced here: 84.4 us
  Pallas kernels  83.6 us (99%)
    pallas_call x1, Pallas kernels, on_device(): pl.pallas_call(kernel, in_specs=[smem, smem] + [anywhere] * 4, out_specs=...  80.9 us
    pallas_call x1, Pallas kernels, on_device(): pl.pallas_call(store_kernel, in_specs=[anywhere] * 4, out_specs=[anywhere...  2.62 us

profile of v6, /device:TPU:2, one launch (start us, length us, event | category | flops | bytes accessed | tf_op | source)
XLA Modules:
  0.0 84.4 jit_solution(3706701186155141254)
XLA Ops:
  0.6 80.9 %packed_attention.1 = (bf16[64,8192]{1,0:T(8,128)(2,1)}, bf16[64,8192]{1,0:T(8,128)(2,1)}, bf16[64,1024]{1,0:T(8,128)(2,1)}, bf16[64,1024]{1,0:T(8,128)(2,1)}) custom-call(s32[16]{0:T(128)} %lens.1, s32[16]{0:T(128)} %share.1, bf16[64,8192]{1,0:T(8,128)(2,1)} %q_ref.1, bf16[64,8192]{1,0:T(8,128)(2,1)} %do_ref.1, bf16[64,1024]{1,0:T(8,128)(2,1)} %k_ref.1, ...), custom_call_target="tpu_custom_call" | custom-call | tf_op jit(solution)/shard_map/packed_attention/pallas_call | solution.py:810
  81.6 2.6 %store_results.1 = (bf16[64,8192]{1,0:T(8,128)(2,1)}, bf16[64,8192]{1,0:T(8,128)(2,1)}, bf16[64,1024]{1,0:T(8,128)(2,1)}, bf16[64,1024]{1,0:T(8,128)(2,1)}) custom-call(bf16[64,8192]{1,0:T(8,128)(2,1)} %get-tuple-element.8.refs_0_, bf16[64,8192]{1,0:T(8,128)(2,1)} %get-tuple-element.9.refs_1_, bf16[64,1024]{1,0:T(8,128)(2,1)} %get-tuple-element.10.refs_2_, ...), custom_call_target="tpu_custom_call" | custom-call | tf_op jit(solution)/shard_map/store_results/pallas_call | solution.py:860
